TPU v7x, 256 devices: a whole 4x4x8 slice. The times are simulated.
256 devices in a mesh: dp: 4 (over y), ctx: 32 (over x, z), chan: 2 (over core).
Axes of the slice: x: 4, y: 4, z: 8, core: 2. Of those that a mesh axis runs over, the one named last changes fastest.
Arguments:
- inputs: bfloat16 [4, 4096, 2, 2048], P('dp', 'ctx', None, 'chan'), may hold values from -6 to 6
- cotangent: bfloat16 [4, 4096, 2048], P('dp', 'ctx'), may hold values from -6 to 6
- out_proj: bfloat16 [2048, 2, 2048], P('dp', None, 'chan'), may hold values from -0.09375 to 0.09375
- modulus: float32 [2048], P('chan'), may hold values from 0.93 to 1, as said below
- phase: float32 [2048], P('chan'), may hold values from -3.140625 to 3.140625
- gain: float32 [2048], P('chan'), may hold values from 0 to 1, as said below
- retain: float32 [4, 4096], P('dp', 'ctx'), may hold values from 0.5 to 1
- doc_starts: int32 [4, 8], P('dp'), may hold values from 0 to 4095, as said below
- row_blocks: int32 [4], P('dp'), may hold values from 1 to 32, as said below
Outputs:
- grad_inputs: bfloat16 [4, 4096, 2, 2048], P('dp', 'ctx', None, 'chan')
- grad_proj: float32 [2048, 2, 2048], P(('dp', 'ctx'), None, 'chan')
- grad_eigen: float32 [2, 2048], P(None, 'chan')
- grad_gain: float32 [2048], P('chan')
Inputs may be any that keep to these rules, and one draw needn't show every extreme that they name: `doc_starts`: the first entry of each row is 0; some row has a document beginning at position 4095. `row_blocks`: one row has all 32 blocks. `modulus`: strictly below 1. `gain`: strictly positive.
All inputs are finite; a program needn't handle non-finite values.
Results may differ from a plain program's by a relative error of at most 0.0029.
Values may be sent and summed in bfloat16 or wider, within the bound.
A program may use at most 128 MiB of HBM per device.

v0:
```python
import jax
import jax.numpy as jnp
from jax import lax
from jax.sharding import PartitionSpec as P


def from_behind(block, axis, distance):
    devices = range(lax.axis_size(axis))
    route = [(i - distance, i) for i in devices if i - distance in devices]
    return lax.ppermute(block, axis, route)


def complex_product(left_real, left_imag, right_real, right_imag):
    return (
        left_real * right_real - left_imag * right_imag,
        left_real * right_imag + left_imag * right_real,
    )


def compose(earlier, latter):
    first_scale_real, first_scale_imag, first_shift_real, first_shift_imag = earlier
    second_scale_real, second_scale_imag, second_shift_real, second_shift_imag = latter
    scale_real, scale_imag = complex_product(
        second_scale_real, second_scale_imag, first_scale_real, first_scale_imag
    )
    moved_real, moved_imag = complex_product(
        second_scale_real, second_scale_imag, first_shift_real, first_shift_imag
    )
    return (scale_real, scale_imag, moved_real + second_shift_real, moved_imag + second_shift_imag)


def body(inputs, cotangent, out_proj, modulus, phase, gain, retain, doc_starts, row_blocks):
    rows, length, _, states = inputs.shape
    width = cotangent.shape[2]
    index = lax.axis_index("ctx")
    position = index * length + jnp.arange(length, dtype=jnp.int32)
    alive = index < row_blocks
    cotangent = jnp.where(alive[:, None, None], cotangent, jnp.zeros_like(cotangent))
    begins = jnp.any(position[None, :, None] == doc_starts[:, None, :], axis=2)
    keep = retain * (1.0 - begins.astype(jnp.float32))
    eigen_real = modulus * jnp.cos(phase)
    eigen_imag = modulus * jnp.sin(phase)
    inputs_real = inputs[:, :, 0, :].astype(jnp.float32)
    inputs_imag = inputs[:, :, 1, :].astype(jnp.float32)
    zeros_state = jnp.zeros((rows, states), jnp.float32)
    step_real = keep[:, :, None] * eigen_real
    step_imag = keep[:, :, None] * eigen_imag
    prefix_real, prefix_imag, local_real, local_imag = lax.associative_scan(
        compose, (step_real, step_imag, gain * inputs_real, gain * inputs_imag), axis=1
    )
    block_real = prefix_real[:, -1]
    block_imag = prefix_imag[:, -1]
    last_real = local_real[:, -1]
    last_imag = local_imag[:, -1]

    def advance_state(step, incoming):
        moved_real, moved_imag = complex_product(block_real, block_imag, incoming[0], incoming[1])
        return from_behind((moved_real + last_real, moved_imag + last_imag), "ctx", 1)

    incoming_real, incoming_imag = lax.fori_loop(
        0, lax.axis_size("ctx") - 1, advance_state, (zeros_state, zeros_state)
    )
    fill_real, fill_imag = complex_product(
        prefix_real, prefix_imag, incoming_real[:, None], incoming_imag[:, None]
    )
    state_real = local_real + fill_real
    state_imag = local_imag + fill_imag
    flat_cotangent = cotangent.reshape(rows * length, width)
    piece = lax.all_gather(out_proj, "dp", axis=0, tiled=True)
    count = piece.shape[0]
    columns = flat_cotangent
    signal = jnp.dot(columns, piece.reshape(count, 2 * states), preferred_element_type=jnp.float32)
    signal_real = signal[:, :states].reshape(rows, length, states)
    signal_imag = signal[:, states:].reshape(rows, length, states)
    next_keep = jnp.concatenate([keep[:, 1:], jnp.ones((rows, 1), jnp.float32)], axis=1)
    back_real = next_keep[:, :, None] * eigen_real
    back_imag = -next_keep[:, :, None] * eigen_imag
    flipped = tuple(
        (jnp.flip(member, axis=1) for member in (back_real, back_imag, signal_real, signal_imag))
    )
    scanned = lax.associative_scan(compose, flipped, axis=1)
    tail_real, tail_imag, adjoint_local_real, adjoint_local_imag = tuple(
        (jnp.flip(member, axis=1) for member in scanned)
    )
    own_real = keep[:, :1] * adjoint_local_real[:, 0]
    own_imag = keep[:, :1] * adjoint_local_imag[:, 0]

    def advance_adjoint(step, incoming):
        moved_real, moved_imag = complex_product(block_real, -block_imag, incoming[0], incoming[1])
        return from_behind((moved_real + own_real, moved_imag + own_imag), "ctx", -1)

    outgoing_real, outgoing_imag = lax.fori_loop(
        0, lax.axis_size("ctx") - 1, advance_adjoint, (zeros_state, zeros_state)
    )
    fix_real, fix_imag = complex_product(
        tail_real, tail_imag, outgoing_real[:, None], outgoing_imag[:, None]
    )
    adjoint_real = adjoint_local_real + fix_real
    adjoint_imag = adjoint_local_imag + fix_imag
    grad_inputs = jnp.stack([gain * adjoint_real, gain * adjoint_imag], axis=2).astype(jnp.bfloat16)
    prior_real = jnp.concatenate([incoming_real[:, None], state_real[:, :-1]], axis=1)
    prior_imag = jnp.concatenate([incoming_imag[:, None], state_imag[:, :-1]], axis=1)
    weighting = keep[:, :, None]
    part_real = jnp.sum(
        weighting * (adjoint_real * prior_real + adjoint_imag * prior_imag), axis=(0, 1)
    )
    part_imag = jnp.sum(
        weighting * (adjoint_imag * prior_real - adjoint_real * prior_imag), axis=(0, 1)
    )
    part_gain = jnp.sum(adjoint_real * inputs_real + adjoint_imag * inputs_imag, axis=(0, 1))
    total_real, total_imag, total_gain = lax.psum((part_real, part_imag, part_gain), ("dp", "ctx"))
    grad_eigen = jnp.stack([total_real, total_imag])
    half_state = (
        jnp.concatenate([state_real, state_imag], axis=2)
        .astype(jnp.bfloat16)
        .reshape(rows * length, 2 * states)
    )
    columns = flat_cotangent
    grad_proj = lax.psum_scatter(
        lax.dot_general(
            columns, half_state, (((0,), (0,)), ((), ())), preferred_element_type=jnp.float32
        ),
        ("dp", "ctx"),
        scatter_dimension=0,
        tiled=True,
    )
    return (grad_inputs, grad_proj.reshape(-1, 2, states), grad_eigen, total_gain)


def solution(mesh):
    return jax.shard_map(
        body,
        mesh=mesh,
        in_specs=(
            P("dp", "ctx", None, "chan"),
            P("dp", "ctx", None),
            P("dp", None, "chan"),
            P("chan"),
            P("chan"),
            P("chan"),
            P("dp", "ctx"),
            P("dp", None),
            P("dp"),
        ),
        out_specs=(
            P("dp", "ctx", None, "chan"),
            P(("dp", "ctx"), None, "chan"),
            P(None, "chan"),
            P("chan"),
        ),
        check_vma=False,
    )
```

profile of v0, /device:TPU:32, one launch (start us, length us, event | category | flops | bytes accessed | tf_op | source)
XLA Modules:
  0.0 1716.9 jit_solution(480149510610174507)
XLA Ops:
  243.4 293.7 %while.27 = (s32[]{:T(128)}, f32[1,1024]{1,0:T(1,128)S(1)}, f32[1,1024]{1,0:T(1,128)S(1)}, f32[1,1024]{1,0:T(1,128)S(1)}, f32[1,1024]{1,0:T(1,128)S(1)}, /*index...) while((s32[]{:T(128)}, f32[1,1024]{1,0:T(1,128)S(1)}, f32[1,1024]{1,0:T(1,128)S(1)}, ...), condition=%wide.region_4.5_spmd, body=%wide.region_3.4_spmd.sunk | while | flops 8194 | bytes 65701 | solution.py:60
  252.8 4.8 collective-permute-start.2
  257.5 4.2 collective-permute-start.3
  263.1 4.2 collective-permute-start.2
  267.3 4.2 collective-permute-start.3
  272.8 4.2 collective-permute-start.2
  320.9 4.2 collective-permute-start.3
  326.4 4.2 collective-permute-start.2
  330.6 4.2 collective-permute-start.3
  336.1 4.2 collective-permute-start.2
  340.3 4.2 collective-permute-start.3
  345.9 4.2 collective-permute-start.2
  350.0 4.0 collective-permute-start.3
  355.6 4.0 collective-permute-start.2
  359.6 4.1 collective-permute-start.3
  365.1 4.1 collective-permute-start.2
  378.7 4.0 collective-permute-start.3
  384.2 4.0 collective-permute-start.2
  388.3 4.0 collective-permute-start.3
  393.8 4.0 collective-permute-start.2
  407.4 4.1 collective-permute-start.3
  412.9 4.1 collective-permute-start.2
  426.5 4.0 collective-permute-start.3
  432.0 4.0 collective-permute-start.2
  436.0 4.0 collective-permute-start.3
  441.6 4.0 collective-permute-start.2
  455.2 4.0 collective-permute-start.3
  460.7 4.0 collective-permute-start.2
  464.7 4.0 collective-permute-start.3
  470.2 4.0 collective-permute-start.2
  474.3 4.0 collective-permute-start.3
  479.8 4.0 collective-permute-start.2
  483.8 4.0 collective-permute-start.3
  489.3 4.0 collective-permute-start.2
  493.4 4.0 collective-permute-start.3
  498.9 4.0 collective-permute-start.2
  502.9 4.1 collective-permute-start.3
  508.5 4.1 collective-permute-start.2
  522.1 4.0 collective-permute-start.3
  527.6 4.0 collective-permute-start.2
  531.6 4.0 collective-permute-start.3
  540.6 8.2 fusion.2
  566.3 10.2 copy.24
  576.5 4.7 fusion.7
  628.0 4.7 rev.26
  720.0 4.7 rev.25
  727.7 283.2 %while.26 = (s32[]{:T(128)}, f32[1,1024]{1,0:T(1,128)S(1)}, f32[1,1024]{1,0:T(1,128)S(1)}, f32[1,1024]{1,0:T(1,128)S(1)}, f32[1,1024]{1,0:T(1,128)S(1)}, /*index...) while((s32[]{:T(128)}, f32[1,1024]{1,0:T(1,128)S(1)}, f32[1,1024]{1,0:T(1,128)S(1)}, ...), condition=%wide.region_2.3_spmd, body=%wide.region_1.2_spmd.sunk | while | flops 8194 | bytes 65701 | solution.py:92
  1014.4 692.8 %all-reduce.112 = (f32[1,1024]{1,0:T(1,128)S(1)}, f32[1,1024]{1,0:T(1,128)S(1)}, f32[1024]{0:T(1024)}) all-reduce(f32[1,1024]{1,0:T(1,128)S(1)} %bitcast.86, f32[1,1024]{1,0:T(1,128)S(1)} %bitcast.85, f32[1024]{0:T(1024)S(1)} %get-tuple-element.144), channel_id=1, replica_groups=mesh['dp'=4,'ctx'=32,'chan'=2] {'dp','ctx'}, use_global_device_ids=true, to_apply=%region_9.10 | all-reduce | flops 3072 | bytes 24576 | tf_op jit(solution)/shard_map/psum | solution.py:111
  (778 shorter events, 808.8 us)
Async XLA Ops:
  8.0 558.3 %all-gather.2.cloned.1.call-start = ((), (), s32[]{:S(2)}) async-start(), calls=%async_computation.1 | async-start | bytes 10485760 | tf_op jit(solution)/shard_map/all_gather | solution.py:69
  8.8 1699.1 %reduce-scatter.2.cloned.1.call-start = ((), (), s32[]{:S(2)}) async-start(), calls=%async_computation.2 | async-start | bytes 16908288 | tf_op jit(solution)/shard_map/reduce_scatter | solution.py:119
  243.4 7.8 collective-permute-start.2
  252.8 9.0 collective-permute-start.2
  263.1 8.4 collective-permute-start.2
  317.1 8.0 collective-permute-start.2
  326.4 8.4 collective-permute-start.2
  336.1 8.4 collective-permute-start.2
  345.9 8.2 collective-permute-start.2
  355.6 8.1 collective-permute-start.2
  365.1 8.1 collective-permute-start.2
  374.7 8.1 collective-permute-start.2
  384.2 8.1 collective-permute-start.2
  393.8 8.1 collective-permute-start.2
  403.4 8.1 collective-permute-start.2
  412.9 8.1 collective-permute-start.2
  422.5 8.0 collective-permute-start.2
  432.0 8.1 collective-permute-start.2
  441.6 8.1 collective-permute-start.2
  451.1 8.1 collective-permute-start.2
  460.7 8.1 collective-permute-start.2
  470.2 8.1 collective-permute-start.2
  479.8 8.1 collective-permute-start.2
  489.3 8.1 collective-permute-start.2
  498.9 8.1 collective-permute-start.2
  508.5 8.1 collective-permute-start.2
  518.0 8.1 collective-permute-start.2
  527.6 8.1 collective-permute-start.2
  848.3 7.6 collective-permute-start
  850.2 7.6 collective-permute-start.1
  867.4 7.7 collective-permute-start
  869.3 7.7 collective-permute-start.1
  888.4 7.6 collective-permute-start.1
  915.2 7.6 collective-permute-start
  917.1 7.6 collective-permute-start.1
  924.7 7.6 collective-permute-start
  934.3 7.6 collective-permute-start
  936.2 7.6 collective-permute-start.1
  943.9 7.6 collective-permute-start
  945.8 7.6 collective-permute-start.1
  963.0 7.6 collective-permute-start
  964.9 7.6 collective-permute-start.1
  972.6 7.6 collective-permute-start
  974.5 7.6 collective-permute-start.1
  982.1 7.6 collective-permute-start
  984.1 7.6 collective-permute-start.1
  1001.2 7.7 collective-permute-start
  1003.2 7.7 collective-permute-start.1
  (102 other events, 2566.7 us)
Sparse Core Ops, SparseCore 0:
  10.7 88.3 all-gather.1
Sparse Core Ops, SparseCore 1:
  548.9 728.9 reduce-scatter.1
where the time goes:
time: 1740 us; the launch traced here: 1720 us
  blocking collectives  693 us (40%)
  starting transfers between devices  363 us (21%)
  local copies, waits for them, and re-layouts  279 us (16%)
  waiting for transfers between devices  212 us (12%)
  other arithmetic  138 us (8%)
    psum x1, blocking collectives, body(): lax.psum((part_real, part_imag, part_gain), ('dp', 'ctx'))  693 us
    ppermute x124, starting transfers between devices, from_behind(): return lax.ppermute(block, axis, route)  363 us
    ppermute x124, waiting for transfers between devices, from_behind(): return lax.ppermute(block, axis, route)  211 us
    slice x91, local copies, waits for them, and re-layouts, body(): lax.associative_scan(compose, (step_real, step_imag, gain * inputs_real,...  110 us
    pad x48, local copies, waits for them, and re-layouts, body(): lax.associative_scan(compose, (step_real, step_imag, gain * inputs_real,...  52.3 us
    pad x48, local copies, waits for them, and re-layouts, body(): scanned = lax.associative_scan(compose, flipped, axis=1)  47 us
    slice x97, local copies, waits for them, and re-layouts, body(): scanned = lax.associative_scan(compose, flipped, axis=1)  37.7 us
  transfers between devices with their start and end apart: 126, of which 93 were waited for; matrix products, arithmetic and copies ran while one was open for 25% of the time, Pallas kernels for 0%

commit v1 on v0

v1 whole, which is shorter than its diff:
```python
import functools

import jax
import jax.numpy as jnp
from jax import lax
from jax.experimental import pallas as pl
from jax.experimental.pallas import tpu as pltpu
from jax.sharding import PartitionSpec as P

MESH = pl.DeviceIdType.MESH
F32 = jnp.float32
BF16 = jnp.bfloat16
LANE = 128
SEGS = 8


def grid_of(ctx):
    z = {32: 8, 4: 2, 8: 4}[ctx]
    return ctx // z, z


def cmul(ar, ai, br, bi):
    return ar * br - ai * bi, ar * bi + ai * br


def wide(row, states):
    return jnp.concatenate([row] * (states // LANE), axis=1)


def lanes_of(j):
    return slice(j * LANE, (j + 1) * LANE)


def nearest_last(n):
    return sorted(range(1, n), key=lambda k: -min(k, n - k))


def kernel(
    dims,
    u_ref, cot_ref, w_ref, mod_ref, mask_ref,
    gin_ref, gproj_ref, gsum_ref,
    ur, ui, st_r, st_i, sg_r, sg_i, seg, carry_f, carry_b,
    cga, cslab, ps_send, ps_recv, half, sga, out_x, recv_x, out_y, recv_y, out_z, recv_z,
    msg_fz, msg_fx, msg_bz, msg_bx, msg_sz, msg_sx, msg_sy,
    slab_s, slab_r, ag_s, ag_r, dd_s, dd_r, ps_s, ps_r, sg_s, sg_rs,
    x_s, x_r, y_s, y_r, z_s, z_r,
    fz_s, fz_r, fx_s, fx_r, bz_s, bz_r, bx_s, bx_r, sz_s, sz_r, sx_s, sx_r, sy_s, sy_r,
):
    ny, nx, nz, nc = dims
    tokens, width = cot_ref.shape
    tiles = ur.shape[0]
    states = tiles * LANE
    steps = tokens // SEGS
    slab = width // ny
    part = width // nc
    y = lax.axis_index("dp")
    ctx = lax.axis_index("ctx")
    c = lax.axis_index("chan")
    x, z = ctx // nz, ctx % nz

    def at_z(other):
        return (y, x * nz + other, c)

    def at_x(other):
        return (y, other * nz + z, c)

    def at_y(other):
        return (other, ctx, c)

    sibling = (y, ctx, 1 - c)
    z_peers = [(z + k) % nz for k in nearest_last(nz)]
    x_peers = [(x + k) % nx for k in nearest_last(nx)]
    y_peers = [(y + k) % ny for k in nearest_last(ny)]

    def copy(src, dst, ssem, rsem, device):
        return pltpu.make_async_remote_copy(
            src_ref=src, dst_ref=dst, send_sem=ssem, recv_sem=rsem,
            device_id=device, device_id_type=MESH,
        )

    barrier = pltpu.get_barrier_semaphore()
    greeted = [at_z(p) for p in z_peers] + [at_x(p) for p in x_peers]
    greeted += [at_y(p) for p in y_peers] + [sibling]
    for device in greeted:
        pl.semaphore_signal(barrier, inc=1, device_id=device, device_id_type=MESH)

    alive = mask_ref[1].astype(BF16)
    for h in range(nc):
        cga[z, h] = cot_ref[:, h * part:(h + 1) * part] * wide(alive, part)
    for j in range(tiles):
        ur[j] = u_ref[0, :, lanes_of(j)].astype(F32)
        ui[j] = u_ref[1, :, lanes_of(j)].astype(F32)
    pl.semaphore_wait(barrier, len(greeted))

    def spread(buf, ssem, rsem, mine, peers, where):
        sends = [copy(buf.at[mine], buf.at[mine], ssem.at[p], rsem.at[mine], where(p)) for p in peers]
        for s in sends:
            s.start()
        return sends

    def collect(buf, ssem, rsem, peers, where):
        for p in peers:
            copy(buf.at[p], buf.at[p], ssem.at[p], rsem.at[p], where(p)).wait_recv()

    pending = []

    def slab_view(at):
        per = ny // nc
        lanes = pl.ds(pl.multiple_of((at % per) * slab, LANE), slab)
        return cga.at[z, at // per, :, lanes]

    for p in y_peers:
        s = copy(slab_view(p), cslab.at[y], slab_s.at[p], slab_r.at[y], at_y(p))
        s.start()
        pending.append(s)

    n_right = nz // 2
    n_left = nz - 1 - n_right

    def ring_send(k, to_right):
        slot = (z - k) % nz if to_right else (z + k) % nz
        other = (z + 1) % nz if to_right else (z - 1) % nz
        sem = ag_s.at[0 if to_right else 1, k]
        s = copy(cga.at[slot, c], cga.at[slot, c], sem, ag_r.at[slot], at_z(other))
        s.start()
        pending.append(s)

    def ring_step(k):
        for to_right, count in ((True, n_right), (False, n_left)):
            if 1 <= k <= count:
                slot = (z - k) % nz if to_right else (z + k) % nz
                view = cga.at[slot, c]
                copy(view, view, ag_s.at[0, 0], ag_r.at[slot], sibling).wait_recv()
                if k < count:
                    ring_send(k, to_right)
                s = copy(view, view, dd_s.at[slot], dd_r.at[slot], sibling)
                s.start()
                pending.append(s)
            elif k == 0 and count > 0:
                ring_send(0, to_right)

    ring_step(0)

    lr1 = mod_ref[0:1]
    li1 = mod_ref[1:2]
    gain1 = mod_ref[2:3]
    shape = (SEGS, states)
    lr = jnp.broadcast_to(lr1, shape)
    li = jnp.broadcast_to(li1, shape)
    gain = jnp.broadcast_to(gain1, shape)

    def power(br, bi, n):
        while n > 1:
            br, bi = cmul(br, bi, br, bi)
            n //= 2
        return br, bi

    seg_r, seg_i = power(lr1, li1, steps)
    blk_r, blk_i = power(seg_r, seg_i, SEGS)
    row_r, row_i = power(blk_r, blk_i, nz)

    def rows(ref, i):
        at = pl.ds(i, SEGS, stride=steps)
        return jnp.concatenate([ref[j, at, :] for j in range(tiles)], axis=1)

    def put_rows(ref, i, value):
        for j in range(tiles):
            ref[j, pl.ds(i, SEGS, stride=steps), :] = value[:, lanes_of(j)]

    def keep_at(i):
        return mask_ref[0, pl.ds(i, SEGS, stride=steps), :]

    def summary(i, held):
        sr, si, kp = held
        k = keep_at(i)
        kk = wide(k, states)
        tr, ti = cmul(lr, li, sr, si)
        return kk * tr + gain * rows(ur, i), kk * ti + gain * rows(ui, i), kp * k

    zero = jnp.zeros(shape, F32)
    sr, si, kp = lax.fori_loop(0, steps, summary, (zero, zero, jnp.ones((SEGS, LANE), F32)))
    seg[0] = sr
    seg[1] = si
    seg[2] = wide(kp, states)

    def chain(hr, hi, sign, hold):
        order = range(SEGS) if sign > 0 else range(SEGS - 1, -1, -1)
        for g in order:
            if hold is not None:
                hold[0, g:g + 1] = hr
                hold[1, g:g + 1] = hi
            pr, pi = cmul(seg_r, sign * seg_i, hr, hi)
            kg = seg[2, g:g + 1]
            hr = kg * pr + seg[0, g:g + 1]
            hi = kg * pi + seg[1, g:g + 1]
        return hr, hi

    one = jnp.ones((1, states), F32)
    nil = jnp.zeros((1, states), F32)

    def across(buf, mine, n, ar, ai, sign, keeps):
        order = range(n) if sign > 0 else range(n - 1, -1, -1)
        hr, hi, pr, pi, kr = nil, nil, one, nil, one[:, :LANE]
        er, ei, qr, qi = nil, nil, one, nil
        for k in order:
            here = k == mine
            er = jnp.where(here, hr, er)
            ei = jnp.where(here, hi, ei)
            qr = jnp.where(here, pr, qr)
            qi = jnp.where(here, pi, qi)
            kw = wide(keeps[k], states)
            mr, mi = cmul(ar, sign * ai, hr, hi)
            hr = kw * mr + buf[k, :, 0:states]
            hi = kw * mi + buf[k, :, states:2 * states]
            mr, mi = cmul(ar, sign * ai, pr, pi)
            pr, pi = kw * mr, kw * mi
            kr = kr * keeps[k]
        return hr, hi, er, ei, qr, qi, kr

    br, bi = chain(nil, nil, 1, None)
    kb = one[:, :LANE]
    for g in range(SEGS):
        kb = kb * seg[2, g:g + 1, 0:LANE]
    msg_fz[z, :, 0:states] = br
    msg_fz[z, :, states:2 * states] = bi
    msg_fz[z, :, 2 * states:] = kb
    pending += spread(msg_fz, fz_s, fz_r, z, z_peers, at_z)
    collect(msg_fz, fz_s, fz_r, z_peers, at_z)
    keeps_z = [msg_fz[k, :, 2 * states:] for k in range(nz)]
    hr, hi, er, ei, qr, qi, kx = across(msg_fz, z, nz, blk_r, blk_i, 1, keeps_z)
    msg_fx[x, :, 0:states] = hr
    msg_fx[x, :, states:2 * states] = hi
    msg_fx[x, :, 2 * states:] = kx
    pending += spread(msg_fx, fx_s, fx_r, x, x_peers, at_x)
    collect(msg_fx, fx_s, fx_r, x_peers, at_x)
    keeps_x = [msg_fx[k, :, 2 * states:] for k in range(nx)]
    _, _, fr, fi, _, _, _ = across(msg_fx, x, nx, row_r, row_i, 1, keeps_x)
    mr, mi = cmul(qr, qi, fr, fi)
    chain(mr + er, mi + ei, 1, carry_f)

    def fill(i, held):
        sr, si = held
        kk = wide(keep_at(i), states)
        tr, ti = cmul(lr, li, sr, si)
        sr = kk * tr + gain * rows(ur, i)
        si = kk * ti + gain * rows(ui, i)
        put_rows(st_r, i, sr)
        put_rows(st_i, i, si)
        return sr, si

    lax.fori_loop(0, steps, fill, (carry_f[0], carry_f[1]))
    for k in range(nz):
        half[k, :, 0:LANE] = st_r[k].astype(BF16)
        half[k, :, LANE:] = st_i[k].astype(BF16)
    for p in z_peers:
        s = copy(half.at[p], sga.at[z], sg_s.at[p], sg_rs.at[z], at_z(p))
        s.start()
        pending.append(s)
    sga[z] = half[z]

    ring_step(1)

    for p in y_peers:
        copy(cslab.at[p], cslab.at[p], slab_s.at[p], slab_r.at[p], at_y(p)).wait_recv()
        for h in range(2):
            ps_send[p, h] = jnp.dot(cslab[p], w_ref[h], preferred_element_type=F32).astype(BF16)
            s = copy(ps_send.at[p, h], ps_recv.at[y, h], ps_s.at[p, h], ps_r.at[y, h], at_y(p))
            s.start()
            pending.append(s)
    own = slab_view(y)[...]
    for h, ref in ((0, sg_r), (1, sg_i)):
        share = jnp.dot(own, w_ref[h], preferred_element_type=F32)
        for j in range(tiles):
            ref[j] = share[:, lanes_of(j)]

    for k in range(2, n_right + 1):
        ring_step(k)
    for k in range(1, nz):
        view = cga.at[(z + k) % nz, 1 - c]
        copy(view, view, dd_s.at[0], dd_r.at[(z + k) % nz], sibling).wait_recv()
    collect(sga, sg_s, sg_rs, z_peers, at_z)

    count = nz * tokens
    state_t = sga[...].reshape(count, 2 * LANE).T
    per = ny // nc
    for q in range(ny):
        lanes = slice((q % per) * slab, (q % per + 1) * slab)
        block = cga[:, q // per, :, lanes].reshape(count, slab)
        grad = jnp.dot(state_t, block, preferred_element_type=F32)
        for k in range(nx):
            out_x[k, q] = grad[:, lanes_of(k)]
    for p in x_peers:
        s = copy(out_x.at[p], recv_x.at[x], x_s.at[p], x_r.at[x], at_x(p))
        s.start()
        pending.append(s)

    for p in y_peers:
        for h, ref in ((0, sg_r), (1, sg_i)):
            view = ps_recv.at[p, h]
            copy(view, view, ps_s.at[p, h], ps_r.at[p, h], at_y(p)).wait_recv()
            for j in range(tiles):
                ref[j] += ps_recv[p, h, :, lanes_of(j)].astype(F32)

    def back_summary(n, held):
        i = steps - 1 - n
        hr, hi = held
        kk = wide(keep_at(i), states)
        tr, ti = cmul(lr, -li, rows(sg_r, i) + hr, rows(sg_i, i) + hi)
        return kk * tr, kk * ti

    hr, hi = lax.fori_loop(0, steps, back_summary, (zero, zero))
    seg[0] = hr
    seg[1] = hi
    br, bi = chain(nil, nil, -1, None)
    msg_bz[z, :, 0:states] = br
    msg_bz[z, :, states:] = bi
    pending += spread(msg_bz, bz_s, bz_r, z, z_peers, at_z)
    collect(msg_bz, bz_s, bz_r, z_peers, at_z)
    hr, hi, er, ei, qr, qi, _ = across(msg_bz, z, nz, blk_r, blk_i, -1, keeps_z)
    msg_bx[x, :, 0:states] = hr
    msg_bx[x, :, states:] = hi
    pending += spread(msg_bx, bx_s, bx_r, x, x_peers, at_x)
    collect(msg_bx, bx_s, bx_r, x_peers, at_x)
    _, _, fr, fi, _, _, _ = across(msg_bx, x, nx, row_r, row_i, -1, keeps_x)
    mr, mi = cmul(qr, qi, fr, fi)
    chain(mr + er, mi + ei, -1, carry_b)

    def adjoint_step(i, held, prior_r, prior_i):
        hr, hi, wr, wi, wg = held
        kk = wide(keep_at(i), states)
        ar = rows(sg_r, i) + hr
        ai = rows(sg_i, i) + hi
        put_rows(sg_r, i, gain * ar)
        put_rows(sg_i, i, gain * ai)
        wr = wr + kk * (ar * prior_r + ai * prior_i)
        wi = wi + kk * (ai * prior_r - ar * prior_i)
        wg = wg + ar * rows(ur, i) + ai * rows(ui, i)
        tr, ti = cmul(lr, -li, ar, ai)
        return kk * tr, kk * ti, wr, wi, wg

    def adjoint(n, held):
        i = steps - 1 - n
        return adjoint_step(i, held, rows(st_r, i - 1), rows(st_i, i - 1))

    held = lax.fori_loop(0, steps - 1, adjoint, (carry_b[0], carry_b[1], zero, zero, zero))
    _, _, wr, wi, wg = adjoint_step(0, held, carry_f[0], carry_f[1])
    for j in range(tiles):
        gin_ref[0, :, lanes_of(j)] = sg_r[j].astype(BF16)
        gin_ref[1, :, lanes_of(j)] = sg_i[j].astype(BF16)

    def put(buf, mine, values):
        for k, value in enumerate(values):
            buf[mine, :, k * states:(k + 1) * states] = value

    def total(buf, n):
        out = buf[0]
        for k in range(1, n):
            out = out + buf[k]
        return out

    put(msg_sz, z, [jnp.sum(w, axis=0, keepdims=True) for w in (wr, wi, wg)])
    pending += spread(msg_sz, sz_s, sz_r, z, z_peers, at_z)

    collect(recv_x, x_s, x_r, x_peers, at_x)
    for q in range(ny):
        grad = out_x[x, q]
        for p in x_peers:
            grad = grad + recv_x[p, q]
        out_y[q] = grad
    for p in y_peers:
        s = copy(out_y.at[p], recv_y.at[y], y_s.at[p], y_r.at[y], at_y(p))
        s.start()
        pending.append(s)

    collect(msg_sz, sz_s, sz_r, z_peers, at_z)
    msg_sx[x] = total(msg_sz, nz)
    pending += spread(msg_sx, sx_s, sx_r, x, x_peers, at_x)
    collect(msg_sx, sx_s, sx_r, x_peers, at_x)
    msg_sy[y] = total(msg_sx, nx)
    pending += spread(msg_sy, sy_s, sy_r, y, y_peers, at_y)

    collect(recv_y, y_s, y_r, y_peers, at_y)
    grad = out_y[y]
    for p in y_peers:
        grad = grad + recv_y[p]
    out_z[...] = grad.T.reshape(out_z.shape)
    for p in z_peers:
        s = copy(out_z.at[p], recv_z.at[z], z_s.at[p], z_r.at[z], at_z(p))
        s.start()
        pending.append(s)
    recv_z[z] = out_z[z]

    collect(msg_sy, sy_s, sy_r, y_peers, at_y)
    gsum_ref[...] = total(msg_sy, ny)

    collect(recv_z, z_s, z_r, z_peers, at_z)
    for k in range(nz):
        for h in range(2):
            gproj_ref[h, :, lanes_of(k)] = recv_z[k, :, lanes_of(h)]

    for s in pending:
        s.wait_send()


def body(dims, inputs, cotangent, out_proj, modulus, phase, gain, retain, doc_starts, row_blocks):
    ny, nx, nz, nc = dims
    _, tokens, _, states = inputs.shape
    width = cotangent.shape[2]
    slab = width // ny
    index = lax.axis_index("ctx")
    position = index * tokens + jnp.arange(tokens, dtype=jnp.int32)
    begins = jnp.any(position[:, None] == doc_starts, axis=1)
    keep = retain[0] * (1.0 - begins.astype(F32))
    alive = (index < row_blocks[0]).astype(F32)
    mask = jnp.stack(
        [jnp.broadcast_to(keep[:, None], (tokens, LANE)), jnp.full((tokens, LANE), alive)]
    )
    coefficients = jnp.stack([modulus * jnp.cos(phase), modulus * jnp.sin(phase), gain])
    drive = inputs[0].transpose(1, 0, 2)
    weight = out_proj.transpose(1, 0, 2)
    rows_z = LANE // nz
    dma = pltpu.SemaphoreType.DMA

    def pair(*shape):
        return [dma(shape), dma(shape)]

    line = 2 * states + LANE
    scratch = [
        *[pltpu.VMEM((states // LANE, tokens, LANE), F32) for _ in range(6)],
        pltpu.VMEM((3, SEGS, states), F32),
        pltpu.VMEM((2, SEGS, states), F32), pltpu.VMEM((2, SEGS, states), F32),
        pltpu.VMEM((nz, nc, tokens, width // nc), BF16),
        pltpu.VMEM((ny, tokens, slab), BF16),
        pltpu.VMEM((ny, 2, tokens, states), BF16), pltpu.VMEM((ny, 2, tokens, states), BF16),
        pltpu.VMEM((nz, tokens, 2 * LANE), BF16), pltpu.VMEM((nz, tokens, 2 * LANE), BF16),
        pltpu.VMEM((nx, ny, 2 * LANE, LANE), F32), pltpu.VMEM((nx, ny, 2 * LANE, LANE), F32),
        pltpu.VMEM((ny, 2 * LANE, LANE), F32), pltpu.VMEM((ny, 2 * LANE, LANE), F32),
        pltpu.VMEM((nz, rows_z, 2 * LANE), F32), pltpu.VMEM((nz, rows_z, 2 * LANE), F32),
        pltpu.VMEM((nz, 1, line), F32), pltpu.VMEM((nx, 1, line), F32),
        pltpu.VMEM((nz, 1, 2 * states), F32), pltpu.VMEM((nx, 1, 2 * states), F32),
        pltpu.VMEM((nz, 1, 3 * states), F32), pltpu.VMEM((nx, 1, 3 * states), F32),
        pltpu.VMEM((ny, 1, 3 * states), F32),
        *pair(ny), dma((2, nz)), dma((nz,)), *pair(nz), *pair(ny, 2), *pair(nz),
        *pair(nx), *pair(ny), *pair(nz),
        *pair(nz), *pair(nx), *pair(nz), *pair(nx), *pair(nz), *pair(nx), *pair(ny),
    ]
    whole = pl.BlockSpec(memory_space=pltpu.VMEM)
    grad_inputs, grad_proj, sums = pl.pallas_call(
        functools.partial(kernel, dims),
        out_shape=(
            jax.ShapeDtypeStruct((2, tokens, states), BF16),
            jax.ShapeDtypeStruct((2, rows_z, states), F32),
            jax.ShapeDtypeStruct((1, 3 * states), F32),
        ),
        in_specs=[whole] * 5,
        out_specs=(whole,) * 3,
        scratch_shapes=scratch,
        compiler_params=pltpu.CompilerParams(
            collective_id=0, has_side_effects=True, vmem_limit_bytes=56 * 1024 * 1024
        ),
    )(drive, cotangent[0], weight, coefficients, mask)
    sums = sums.reshape(3, states)
    return (
        grad_inputs.transpose(1, 0, 2)[None],
        grad_proj.transpose(1, 0, 2),
        sums[:2],
        sums[2],
    )


def solution(mesh):
    sizes = mesh.shape
    nx, nz = grid_of(sizes["ctx"])
    dims = (sizes["dp"], nx, nz, sizes["chan"])
    return jax.shard_map(
        functools.partial(body, dims),
        mesh=mesh,
        in_specs=(
            P("dp", "ctx", None, "chan"),
            P("dp", "ctx", None),
            P("dp", None, "chan"),
            P("chan"),
            P("chan"),
            P("chan"),
            P("dp", "ctx"),
            P("dp", None),
            P("dp"),
        ),
        out_specs=(
            P("dp", "ctx", None, "chan"),
            P(("dp", "ctx"), None, "chan"),
            P(None, "chan"),
            P("chan"),
        ),
        check_vma=False,
    )
```

time: 1740 us -> 119 us (0.07); the launches traced: 1720 us -> 117 us
  blocking collectives: 693 us -> 0 us
  starting transfers between devices: 363 us -> 0 us
  local copies, waits for them, and re-layouts: 279 us -> 12.9 us
  waiting for transfers between devices: 212 us -> 0 us
  other arithmetic: 138 us -> 3.46 us
  Pallas kernels: 0 us -> 99.8 us
    psum x1 -> x0, blocking collectives: 693 us -> none  [body(): lax.psum((part_real, part_imag, part_gain), ('dp', 'ctx'))]
    ppermute x124 -> x0, starting transfers between devices: 363 us -> none  [from_behind(): return lax.ppermute(block, axis, route)]
    ppermute x124 -> x0, waiting for transfers between devices: 211 us -> none  [from_behind(): return lax.ppermute(block, axis, route)]
    slice x191 -> x3, local copies, waits for them, and re-layouts: 150 us -> 2.59 us  [the longest x2 1.33 us: body(): sums[:2]]
    pallas_call x0 -> x1, Pallas kernels: none -> 99.8 us  [body(): pl.pallas_call(functools.partial(kernel, dims), out_shape=(jax.ShapeDtype...]
    pad x96 -> x0, local copies, waits for them, and re-layouts: 99.3 us -> none  [the longest x48 52.3 us: body(): lax.associative_scan(compose, (step_real, step_imag, gain * inputs_real,...]
    add x149 -> x1, other arithmetic: 80.8 us -> 0.01 us  [body(): position = index * tokens + jnp.arange(tokens, dtype=jnp.int32)]
    concatenate x50 -> x0, other arithmetic: 41 us -> none  [the longest x24 20.7 us: body(): scanned = lax.associative_scan(compose, flipped, axis=1)]
  transfers between devices with their start and end apart: 126 -> 0, of which waited for: 93 -> 0; matrix products, arithmetic and copies ran while one was open for 25% -> 0% of each run, Pallas kernels for 0% -> 0%
where the time goes in v1:
time: 119 us; the launch traced here: 117 us
  Pallas kernels  99.8 us (84%)
  local copies, waits for them, and re-layouts  12.9 us (11%)
  other arithmetic  3.46 us (3%)
  between operations  1.31 us (1%)
    pallas_call x1, Pallas kernels, body(): pl.pallas_call(functools.partial(kernel, dims), out_shape=(jax.ShapeDtype...  99.8 us
    unnamed x4, local copies, waits for them, and re-layouts  9.55 us

profile of v1, /device:TPU:32, one launch (start us, length us, event | category | flops | bytes accessed | tf_op | source)
XLA Modules:
  0.0 117.5 jit_solution(9914057323460377366)
XLA Ops:
  1.3 0.7 compare_reduce_fusion
  2.0 0.7 bitcast_multiply_fusion
  2.7 0.7 cosine_multiply_fusion
  3.4 1.3 %pad_maximum_fusion.mod_ref = f32[3,1024]{1,0:T(4,128)} fusion(f32[1,1024]{1,0:T(1,128)} %bitcast.29, f32[1,1024]{1,0:T(1,128)S(1)} %bitcast.28, f32[1,1024]{1,0:T(1,128)S(1)} %bitcast.27), kind=kLoop, calls=%fused_computation.2 | loop fusion | flops 6144 | bytes 24576 | tf_op jit(solution)/shard_map/stack | solution.py:418
  4.7 0.1 stack_broadcast_in_dim.2
  4.8 0.7 stack.19.mask_ref
  5.5 2.0 %copy.24 = bf16[1,128,2,1024]{3,1,2,0:T(8,128)(2,1)} copy(bf16[1,128,2,1024]{3,2,1,0:T(2,128)(2,1)} %param.9) | data formatting | bytes 1048576 | tf_op args[0]
  7.4 3.6 %copy.23 = bf16[512,2,1024]{2,0,1:T(8,128)(2,1)} copy(bf16[512,2,1024]{2,1,0:T(2,128)(2,1)} %param.11) | data formatting | bytes 4194304 | tf_op args[2]
  11.0 99.8 %shard_map.120 = (bf16[2,128,1024]{2,1,0:T(8,128)(2,1)}, f32[2,16,1024]{2,1,0:T(8,128)}, f32[1,3072]{1,0:T(1,128)}) custom-call(bf16[2,128,1024]{2,1,0:T(8,128)(2,1)} %bitcast.23, bf16[128,2048]{1,0:T(8,128)(2,1)} %bitcast.24, bf16[2,512,1024]{2,1,0:T(8,128)(2,1)} %bitcast.22, f32[3,1024]{1,0:T(4,128)} %pad_maximum_fusion.mod_ref, f32[2,128,128]{2,1,0:T(8,128)} %stack.19.mask_ref), custom_call_target="tpu_custom_call" | custom-call | tf_op jit(solution)/shard_map/pallas_call | solution.py:448
  110.8 2.4 %copy.19 = bf16[1,128,2,1024]{3,2,1,0:T(2,128)(2,1)} copy(bf16[1,128,2,1024]{3,1,2,0:T(8,128)(2,1)} %bitcast.25) | data formatting | bytes 1048576
  113.2 1.7 %copy.20 = f32[16,2,1024]{2,1,0:T(2,128)} copy(f32[16,2,1024]{2,0,1:T(8,128)} %bitcast.26) | data formatting | bytes 262144
  114.9 1.3 %slice.12 = f32[1,1024]{1,0:T(1,128)} slice(f32[1,3072]{1,0:T(1,128)} %get-tuple-element.9), slice={[0:1], [2048:3072]} | slice | bytes 8192 | tf_op jit(solution)/shard_map/slice | solution.py:467
  116.1 0.7 slice_reduce_fusion
  116.9 0.6 slice.11
  (1 shorter events, 0.0 us)

commit v2 on v1

--- a/solution.py
+++ b/solution.py
@@ -37,22 +37,23 @@
 
 def kernel(
     dims,
-    u_ref, cot_ref, w_ref, mod_ref, mask_ref,
-    gin_ref, gproj_ref, gsum_ref,
+    starts_ref, blocks_ref, mod_ref, phase_ref, gain_ref, retain_ref, u_hbm, cot_hbm, w_hbm,
+    gin_ref, gproj_ref, geig_ref, ggain_ref,
+    u_raw, cot_raw, w_raw, w_wide, w_ref, mask,
     ur, ui, st_r, st_i, sg_r, sg_i, seg, carry_f, carry_b,
-    cga, cslab, ps_send, ps_recv, half, sga, out_x, recv_x, out_y, recv_y, out_z, recv_z,
+    cga, cslab, ps_send, ps_recv, half, sga, grads, out_x, recv_x, out_y, recv_y, out_z, recv_z,
     msg_fz, msg_fx, msg_bz, msg_bx, msg_sz, msg_sx, msg_sy,
-    slab_s, slab_r, ag_s, ag_r, dd_s, dd_r, ps_s, ps_r, sg_s, sg_rs,
+    load_s, slab_s, slab_r, ag_s, ag_r, dd_s, dd_r, ps_s, ps_r, sg_s, sg_rs,
     x_s, x_r, y_s, y_r, z_s, z_r,
     fz_s, fz_r, fx_s, fx_r, bz_s, bz_r, bx_s, bx_r, sz_s, sz_r, sx_s, sx_r, sy_s, sy_r,
 ):
     ny, nx, nz, nc = dims
-    tokens, width = cot_ref.shape
+    tokens, width = cot_raw.shape
     tiles = ur.shape[0]
     states = tiles * LANE
     steps = tokens // SEGS
     slab = width // ny
-    part = width // nc
+    stages = ny // nc
     y = lax.axis_index("dp")
     ctx = lax.axis_index("ctx")
     c = lax.axis_index("chan")
@@ -83,13 +84,24 @@
     greeted += [at_y(p) for p in y_peers] + [sibling]
     for device in greeted:
         pl.semaphore_signal(barrier, inc=1, device_id=device, device_id_type=MESH)
-
-    alive = mask_ref[1].astype(BF16)
-    for h in range(nc):
-        cga[z, h] = cot_ref[:, h * part:(h + 1) * part] * wide(alive, part)
-    for j in range(tiles):
-        ur[j] = u_ref[0, :, lanes_of(j)].astype(F32)
-        ui[j] = u_ref[1, :, lanes_of(j)].astype(F32)
+    load_cot = pltpu.make_async_copy(cot_hbm, cot_raw, load_s.at[0])
+    load_u = pltpu.make_async_copy(u_hbm, u_raw, load_s.at[1])
+    load_w = pltpu.make_async_copy(w_hbm, w_raw, load_s.at[2])
+    load_cot.start()
+    load_u.start()
+    load_w.start()
+
+    row = lax.broadcasted_iota(jnp.int32, (1, tokens), 1) + ctx * tokens
+    keep = retain_ref[...]
+    for k in range(starts_ref.shape[1]):
+        keep = jnp.where(row == starts_ref[0, k], 0.0, keep)
+    mask[...] = jnp.broadcast_to(keep, (LANE, tokens)).T
+
+    alive = jnp.where(ctx < blocks_ref[0], 1.0, 0.0).astype(F32)
+    alive = jnp.full((tokens, slab), alive, F32).astype(BF16)
+    load_cot.wait()
+    for q in range(ny):
+        cga[z, q] = cot_raw[:, q * slab:(q + 1) * slab] * alive
     pl.semaphore_wait(barrier, len(greeted))
 
     def spread(buf, ssem, rsem, mine, peers, where):
@@ -104,50 +116,53 @@
 
     pending = []
 
-    def slab_view(at):
-        per = ny // nc
-        lanes = pl.ds(pl.multiple_of((at % per) * slab, LANE), slab)
-        return cga.at[z, at // per, :, lanes]
-
     for p in y_peers:
-        s = copy(slab_view(p), cslab.at[y], slab_s.at[p], slab_r.at[y], at_y(p))
+        s = copy(cga.at[z, p], cslab.at[y], slab_s.at[p], slab_r.at[y], at_y(p))
         s.start()
         pending.append(s)
 
     n_right = nz // 2
     n_left = nz - 1 - n_right
 
-    def ring_send(k, to_right):
-        slot = (z - k) % nz if to_right else (z + k) % nz
-        other = (z + 1) % nz if to_right else (z - 1) % nz
-        sem = ag_s.at[0 if to_right else 1, k]
-        s = copy(cga.at[slot, c], cga.at[slot, c], sem, ag_r.at[slot], at_z(other))
-        s.start()
-        pending.append(s)
-
-    def ring_step(k):
-        for to_right, count in ((True, n_right), (False, n_left)):
+    def ring_step(stage, k):
+        q = stage * nc + c
+        for way, count in ((0, n_right), (1, n_left)):
+            sign = -1 if way == 0 else 1
+            slot = (z + sign * k) % nz
+            view = cga.at[slot, q]
             if 1 <= k <= count:
-                slot = (z - k) % nz if to_right else (z + k) % nz
-                view = cga.at[slot, c]
-                copy(view, view, ag_s.at[0, 0], ag_r.at[slot], sibling).wait_recv()
-                if k < count:
-                    ring_send(k, to_right)
-                s = copy(view, view, dd_s.at[slot], dd_r.at[slot], sibling)
+                copy(view, view, ag_s.at[stage, way, 0], ag_r.at[stage, slot], sibling).wait_recv()
+            if k < count:
+                s = copy(view, view, ag_s.at[stage, way, k], ag_r.at[stage, slot], at_z((z - sign) % nz))
                 s.start()
                 pending.append(s)
-            elif k == 0 and count > 0:
-                ring_send(0, to_right)
-
-    ring_step(0)
-
-    lr1 = mod_ref[0:1]
-    li1 = mod_ref[1:2]
-    gain1 = mod_ref[2:3]
+            if 1 <= k <= count:
+                s = copy(view, view, dd_s.at[stage, slot], dd_r.at[stage, slot], sibling)
+                s.start()
+                pending.append(s)
+
+    def ring_end(stage):
+        q = stage * nc + 1 - c
+        for k in range(1, nz):
+            slot = (z + k) % nz
+            view = cga.at[slot, q]
+            copy(view, view, dd_s.at[stage, slot], dd_r.at[stage, slot], sibling).wait_recv()
+
+    todo = [(stage, k) for stage in range(stages) for k in range(n_right + 1)]
+
+    def advance(count=1, stage=None):
+        while todo and (count > 0 or (stage is not None and todo[0][0] <= stage)):
+            ring_step(*todo.pop(0))
+            count -= 1
+
+    advance()
+
+    lr1 = mod_ref[...] * jnp.cos(phase_ref[...])
+    li1 = mod_ref[...] * jnp.sin(phase_ref[...])
     shape = (SEGS, states)
     lr = jnp.broadcast_to(lr1, shape)
     li = jnp.broadcast_to(li1, shape)
-    gain = jnp.broadcast_to(gain1, shape)
+    gain = jnp.broadcast_to(gain_ref[...], shape)
 
     def power(br, bi, n):
         while n > 1:
@@ -159,6 +174,12 @@
     blk_r, blk_i = power(seg_r, seg_i, SEGS)
     row_r, row_i = power(blk_r, blk_i, nz)
 
+    load_u.wait()
+    drive = u_raw[...].astype(F32)
+    for j in range(tiles):
+        ur[j] = drive[:, 0, lanes_of(j)]
+        ui[j] = drive[:, 1, lanes_of(j)]
+
     def rows(ref, i):
         at = pl.ds(i, SEGS, stride=steps)
         return jnp.concatenate([ref[j, at, :] for j in range(tiles)], axis=1)
@@ -168,7 +189,7 @@
             ref[j, pl.ds(i, SEGS, stride=steps), :] = value[:, lanes_of(j)]
 
     def keep_at(i):
-        return mask_ref[0, pl.ds(i, SEGS, stride=steps), :]
+        return mask[pl.ds(i, SEGS, stride=steps), :]
 
     def summary(i, held):
         sr, si, kp = held
@@ -225,6 +246,22 @@
     msg_fz[z, :, states:2 * states] = bi
     msg_fz[z, :, 2 * states:] = kb
     pending += spread(msg_fz, fz_s, fz_r, z, z_peers, at_z)
+
+    load_w.wait()
+    depth = w_wide.shape[1]
+
+    def part_weights(n, carry):
+        at = pl.ds(pl.multiple_of(n * depth, depth), depth)
+        block = w_raw[at].astype(F32)
+        w_wide[0] = block[:, 0, :]
+        w_wide[1] = block[:, 1, :]
+        w_ref[0, at, :] = w_wide[0].astype(BF16)
+        w_ref[1, at, :] = w_wide[1].astype(BF16)
+        return carry
+
+    lax.fori_loop(0, slab // depth, part_weights, 0)
+    advance()
+
     collect(msg_fz, fz_s, fz_r, z_peers, at_z)
     keeps_z = [msg_fz[k, :, 2 * states:] for k in range(nz)]
     hr, hi, er, ei, qr, qi, kx = across(msg_fz, z, nz, blk_r, blk_i, 1, keeps_z)
@@ -232,6 +269,16 @@
     msg_fx[x, :, states:2 * states] = hi
     msg_fx[x, :, 2 * states:] = kx
     pending += spread(msg_fx, fx_s, fx_r, x, x_peers, at_x)
+
+    for p in y_peers:
+        copy(cslab.at[p], cslab.at[p], slab_s.at[p], slab_r.at[p], at_y(p)).wait_recv()
+        for h in range(2):
+            ps_send[p, h] = jnp.dot(cslab[p], w_ref[h], preferred_element_type=F32).astype(BF16)
+            s = copy(ps_send.at[p, h], ps_recv.at[y, h], ps_s.at[p, h], ps_r.at[y, h], at_y(p))
+            s.start()
+            pending.append(s)
+    advance()
+
     collect(msg_fx, fx_s, fx_r, x_peers, at_x)
     keeps_x = [msg_fx[k, :, 2 * states:] for k in range(nx)]
     _, _, fr, fi, _, _, _ = across(msg_fx, x, nx, row_r, row_i, 1, keeps_x)
@@ -258,41 +305,34 @@
         pending.append(s)
     sga[z] = half[z]
 
-    ring_step(1)
-
-    for p in y_peers:
-        copy(cslab.at[p], cslab.at[p], slab_s.at[p], slab_r.at[p], at_y(p)).wait_recv()
-        for h in range(2):
-            ps_send[p, h] = jnp.dot(cslab[p], w_ref[h], preferred_element_type=F32).astype(BF16)
-            s = copy(ps_send.at[p, h], ps_recv.at[y, h], ps_s.at[p, h], ps_r.at[y, h], at_y(p))
-            s.start()
-            pending.append(s)
-    own = slab_view(y)[...]
+    own = cga[z, y]
     for h, ref in ((0, sg_r), (1, sg_i)):
         share = jnp.dot(own, w_ref[h], preferred_element_type=F32)
         for j in range(tiles):
             ref[j] = share[:, lanes_of(j)]
-
-    for k in range(2, n_right + 1):
-        ring_step(k)
-    for k in range(1, nz):
-        view = cga.at[(z + k) % nz, 1 - c]
-        copy(view, view, dd_s.at[0], dd_r.at[(z + k) % nz], sibling).wait_recv()
+    advance(0, 0)
+    advance()
+
+    def project(stage):
+        count = nz * tokens
+        state_t = sga[...].reshape(count, 2 * LANE).T
+        slabs = range(stage * nc, (stage + 1) * nc)
+        for q in slabs:
+            block = cga[:, q].reshape(count, slab)
+            grad = jnp.dot(state_t, block, preferred_element_type=F32)
+            for k in range(nx):
+                grads[q, k] = grad[:, lanes_of(k)]
+                out_x[k, q] = grad[:, lanes_of(k)].astype(BF16)
+        at = pl.ds(stage * nc, nc)
+        for p in x_peers:
+            s = copy(out_x.at[p, at], recv_x.at[x, at], x_s.at[stage, p], x_r.at[stage, x], at_x(p))
+            s.start()
+            pending.append(s)
+
+    ring_end(0)
     collect(sga, sg_s, sg_rs, z_peers, at_z)
-
-    count = nz * tokens
-    state_t = sga[...].reshape(count, 2 * LANE).T
-    per = ny // nc
-    for q in range(ny):
-        lanes = slice((q % per) * slab, (q % per + 1) * slab)
-        block = cga[:, q // per, :, lanes].reshape(count, slab)
-        grad = jnp.dot(state_t, block, preferred_element_type=F32)
-        for k in range(nx):
-            out_x[k, q] = grad[:, lanes_of(k)]
-    for p in x_peers:
-        s = copy(out_x.at[p], recv_x.at[x], x_s.at[p], x_r.at[x], at_x(p))
-        s.start()
-        pending.append(s)
+    project(0)
+    advance()
 
     for p in y_peers:
         for h, ref in ((0, sg_r), (1, sg_i)):
@@ -315,11 +355,13 @@
     msg_bz[z, :, 0:states] = br
     msg_bz[z, :, states:] = bi
     pending += spread(msg_bz, bz_s, bz_r, z, z_peers, at_z)
+    advance()
     collect(msg_bz, bz_s, bz_r, z_peers, at_z)
     hr, hi, er, ei, qr, qi, _ = across(msg_bz, z, nz, blk_r, blk_i, -1, keeps_z)
     msg_bx[x, :, 0:states] = hr
     msg_bx[x, :, states:] = hi
     pending += spread(msg_bx, bx_s, bx_r, x, x_peers, at_x)
+    advance()
     collect(msg_bx, bx_s, bx_r, x_peers, at_x)
     _, _, fr, fi, _, _, _ = across(msg_bx, x, nx, row_r, row_i, -1, keeps_x)
     mr, mi = cmul(qr, qi, fr, fi)
@@ -344,9 +386,6 @@
 
     held = lax.fori_loop(0, steps - 1, adjoint, (carry_b[0], carry_b[1], zero, zero, zero))
     _, _, wr, wi, wg = adjoint_step(0, held, carry_f[0], carry_f[1])
-    for j in range(tiles):
-        gin_ref[0, :, lanes_of(j)] = sg_r[j].astype(BF16)
-        gin_ref[1, :, lanes_of(j)] = sg_i[j].astype(BF16)
 
     def put(buf, mine, values):
         for k, value in enumerate(values):
@@ -361,20 +400,34 @@
     put(msg_sz, z, [jnp.sum(w, axis=0, keepdims=True) for w in (wr, wi, wg)])
     pending += spread(msg_sz, sz_s, sz_r, z, z_peers, at_z)
 
-    collect(recv_x, x_s, x_r, x_peers, at_x)
+    for stage in range(1, stages):
+        advance(0, stage)
+        ring_end(stage)
+        project(stage)
+
+    collect(msg_sz, sz_s, sz_r, z_peers, at_z)
+    msg_sx[x] = total(msg_sz, nz)
+    pending += spread(msg_sx, sx_s, sx_r, x, x_peers, at_x)
+
+    for j in range(tiles):
+        gin_ref[:, 0, lanes_of(j)] = sg_r[j].astype(BF16)
+        gin_ref[:, 1, lanes_of(j)] = sg_i[j].astype(BF16)
+
+    for stage in range(stages):
+        at = pl.ds(stage * nc, nc)
+        for p in x_peers:
+            view = recv_x.at[p, at]
+            copy(view, view, x_s.at[stage, p], x_r.at[stage, p], at_x(p)).wait_recv()
     for q in range(ny):
-        grad = out_x[x, q]
+        grad = grads[q, x]
         for p in x_peers:
-            grad = grad + recv_x[p, q]
+            grad = grad + recv_x[p, q].astype(F32)
         out_y[q] = grad
     for p in y_peers:
         s = copy(out_y.at[p], recv_y.at[y], y_s.at[p], y_r.at[y], at_y(p))
         s.start()
         pending.append(s)
 
-    collect(msg_sz, sz_s, sz_r, z_peers, at_z)
-    msg_sx[x] = total(msg_sz, nz)
-    pending += spread(msg_sx, sx_s, sx_r, x, x_peers, at_x)
     collect(msg_sx, sx_s, sx_r, x_peers, at_x)
     msg_sy[y] = total(msg_sx, nx)
     pending += spread(msg_sy, sy_s, sy_r, y, y_peers, at_y)
@@ -391,12 +444,15 @@
     recv_z[z] = out_z[z]
 
     collect(msg_sy, sy_s, sy_r, y_peers, at_y)
-    gsum_ref[...] = total(msg_sy, ny)
+    sums = total(msg_sy, ny)
+    geig_ref[0:1] = sums[:, 0:states]
+    geig_ref[1:2] = sums[:, states:2 * states]
+    ggain_ref[...] = sums[:, 2 * states:]
 
     collect(recv_z, z_s, z_r, z_peers, at_z)
     for k in range(nz):
         for h in range(2):
-            gproj_ref[h, :, lanes_of(k)] = recv_z[k, :, lanes_of(h)]
+            gproj_ref[:, h, lanes_of(k)] = recv_z[k, :, lanes_of(h)]
 
     for s in pending:
         s.wait_send()
@@ -407,17 +463,7 @@
     _, tokens, _, states = inputs.shape
     width = cotangent.shape[2]
     slab = width // ny
-    index = lax.axis_index("ctx")
-    position = index * tokens + jnp.arange(tokens, dtype=jnp.int32)
-    begins = jnp.any(position[:, None] == doc_starts, axis=1)
-    keep = retain[0] * (1.0 - begins.astype(F32))
-    alive = (index < row_blocks[0]).astype(F32)
-    mask = jnp.stack(
-        [jnp.broadcast_to(keep[:, None], (tokens, LANE)), jnp.full((tokens, LANE), alive)]
-    )
-    coefficients = jnp.stack([modulus * jnp.cos(phase), modulus * jnp.sin(phase), gain])
-    drive = inputs[0].transpose(1, 0, 2)
-    weight = out_proj.transpose(1, 0, 2)
+    stages = ny // nc
     rows_z = LANE // nz
     dma = pltpu.SemaphoreType.DMA
 
@@ -426,46 +472,53 @@
 
     line = 2 * states + LANE
     scratch = [
+        pltpu.VMEM((tokens, 2, states), BF16),
+        pltpu.VMEM((tokens, width), BF16),
+        pltpu.VMEM((slab, 2, states), BF16),
+        pltpu.VMEM((2, LANE, states), F32),
+        pltpu.VMEM((2, slab, states), BF16),
+        pltpu.VMEM((tokens, LANE), F32),
         *[pltpu.VMEM((states // LANE, tokens, LANE), F32) for _ in range(6)],
         pltpu.VMEM((3, SEGS, states), F32),
         pltpu.VMEM((2, SEGS, states), F32), pltpu.VMEM((2, SEGS, states), F32),
-        pltpu.VMEM((nz, nc, tokens, width // nc), BF16),
+        pltpu.VMEM((nz, ny, tokens, slab), BF16),
         pltpu.VMEM((ny, tokens, slab), BF16),
         pltpu.VMEM((ny, 2, tokens, states), BF16), pltpu.VMEM((ny, 2, tokens, states), BF16),
         pltpu.VMEM((nz, tokens, 2 * LANE), BF16), pltpu.VMEM((nz, tokens, 2 * LANE), BF16),
-        pltpu.VMEM((nx, ny, 2 * LANE, LANE), F32), pltpu.VMEM((nx, ny, 2 * LANE, LANE), F32),
+        pltpu.VMEM((ny, nx, 2 * LANE, LANE), F32),
+        pltpu.VMEM((nx, ny, 2 * LANE, LANE), BF16), pltpu.VMEM((nx, ny, 2 * LANE, LANE), BF16),
         pltpu.VMEM((ny, 2 * LANE, LANE), F32), pltpu.VMEM((ny, 2 * LANE, LANE), F32),
         pltpu.VMEM((nz, rows_z, 2 * LANE), F32), pltpu.VMEM((nz, rows_z, 2 * LANE), F32),
         pltpu.VMEM((nz, 1, line), F32), pltpu.VMEM((nx, 1, line), F32),
         pltpu.VMEM((nz, 1, 2 * states), F32), pltpu.VMEM((nx, 1, 2 * states), F32),
         pltpu.VMEM((nz, 1, 3 * states), F32), pltpu.VMEM((nx, 1, 3 * states), F32),
         pltpu.VMEM((ny, 1, 3 * states), F32),
-        *pair(ny), dma((2, nz)), dma((nz,)), *pair(nz), *pair(ny, 2), *pair(nz),
-        *pair(nx), *pair(ny), *pair(nz),
+        dma((3,)), *pair(ny), dma((stages, 2, nz)), dma((stages, nz)), *pair(stages, nz),
+        *pair(ny, 2), *pair(nz), *pair(stages, nx), *pair(ny), *pair(nz),
         *pair(nz), *pair(nx), *pair(nz), *pair(nx), *pair(nz), *pair(nx), *pair(ny),
     ]
-    whole = pl.BlockSpec(memory_space=pltpu.VMEM)
-    grad_inputs, grad_proj, sums = pl.pallas_call(
+    vmem = pl.BlockSpec(memory_space=pltpu.VMEM)
+    smem = pl.BlockSpec(memory_space=pltpu.SMEM)
+    hbm = pl.BlockSpec(memory_space=pl.ANY)
+    grad_inputs, grad_proj, grad_eigen, grad_gain = pl.pallas_call(
         functools.partial(kernel, dims),
         out_shape=(
-            jax.ShapeDtypeStruct((2, tokens, states), BF16),
-            jax.ShapeDtypeStruct((2, rows_z, states), F32),
-            jax.ShapeDtypeStruct((1, 3 * states), F32),
+            jax.ShapeDtypeStruct((tokens, 2, states), BF16),
+            jax.ShapeDtypeStruct((rows_z, 2, states), F32),
+            jax.ShapeDtypeStruct((2, states), F32),
+            jax.ShapeDtypeStruct((1, states), F32),
         ),
-        in_specs=[whole] * 5,
-        out_specs=(whole,) * 3,
+        in_specs=[smem, smem, vmem, vmem, vmem, vmem, hbm, hbm, hbm],
+        out_specs=(vmem,) * 4,
         scratch_shapes=scratch,
         compiler_params=pltpu.CompilerParams(
             collective_id=0, has_side_effects=True, vmem_limit_bytes=56 * 1024 * 1024
         ),
-    )(drive, cotangent[0], weight, coefficients, mask)
-    sums = sums.reshape(3, states)
-    return (
-        grad_inputs.transpose(1, 0, 2)[None],
-        grad_proj.transpose(1, 0, 2),
-        sums[:2],
-        sums[2],
+    )(
+        doc_starts, row_blocks, modulus[None], phase[None], gain[None], retain,
+        inputs[0], cotangent[0], out_proj,
     )
+    return grad_inputs[None], grad_proj, grad_eigen, grad_gain[0]
 
 
 def solution(mesh):

time: 119 us -> 91 us (0.76)
  Pallas kernels: 99.8 us -> 81.9 us
  local copies, waits for them, and re-layouts: 12.9 us -> 6.32 us
  other arithmetic: 3.46 us -> 0 us
    pallas_call x1, Pallas kernels: 99.8 us -> 81.9 us  [body(): pl.pallas_call(functools.partial(kernel, dims), out_shape=(jax.ShapeDtype...]
    unnamed x4, local copies, waits for them, and re-layouts: 9.55 us -> 6.32 us
    slice x3 -> x0, local copies, waits for them, and re-layouts: 2.59 us -> none  [the longest x2 1.33 us: body(): sums[:2]]
    mul x2 -> x0, other arithmetic: 1.4 us -> none  [the longest x1 0.74 us: body(): modulus * jnp.cos(phase)]
    another operation x1 -> x0, other arithmetic: 1.31 us -> none  [body(): jnp.stack([modulus * jnp.cos(phase), modulus * jnp.sin(phase), gain])]
where the time goes in v2:
time: 91 us; the launch traced here: 89.5 us
  Pallas kernels  81.9 us (90%)
  local copies, waits for them, and re-layouts  6.32 us (7%)
  between operations  1.29 us (1%)
    pallas_call x1, Pallas kernels, body(): pl.pallas_call(functools.partial(kernel, dims), out_shape=(jax.ShapeDtype...  81.9 us
    unnamed x4, local copies, waits for them, and re-layouts  6.32 us

profile of v2, /device:TPU:32, one launch (start us, length us, event | category | flops | bytes accessed | tf_op | source)
XLA Modules:
  0.0 89.5 jit_solution(385428809101788433)
XLA Ops:
  1.3 81.9 %shard_map.120 = (bf16[128,2,1024]{2,1,0:T(2,128)(2,1)}, f32[16,2,1024]{2,1,0:T(2,128)}, f32[2,1024]{1,0:T(2,128)}, f32[1,1024]{1,0:T(1,128)}) custom-call(s32[1,8]{1,0:T(1,128)} %starts_ref.1, s32[1]{0:T(128)S(6)} %copy.17.blocks_ref, f32[1,1024]{1,0:T(1,128)} %bitcast.10, f32[1,1024]{1,0:T(1,128)} %bitcast.11, f32[1,1024]{1,0:T(1,128)} %bitcast.12, ...), custom_call_target="tpu_custom_call" | custom-call | tf_op jit(solution)/shard_map/pallas_call | solution.py:503
  83.2 2.2 %copy.18 = bf16[1,128,2,1024]{3,2,1,0:T(2,128)(2,1)} copy(bf16[1,128,2,1024]{3,2,1,0:T(2,128)(2,1)} %bitcast.9) | data formatting | bytes 1048576
  85.4 1.6 %copy.19 = f32[16,2,1024]{2,1,0:T(2,128)} copy(f32[16,2,1024]{2,1,0:T(2,128)} %get-tuple-element.17) | data formatting | bytes 262144
  87.0 1.3 %copy.20 = f32[2,1024]{1,0:T(2,128)} copy(f32[2,1024]{1,0:T(2,128)} %get-tuple-element.18) | data formatting | bytes 16384
  88.3 1.3 %copy.21 = f32[1024]{0:T(1024)} copy(f32[1024]{0:T(1024)} %bitcast.13) | data formatting | bytes 8192

commit v3 on v2

v3 whole, which is shorter than its diff:
```python
import functools

import jax
import jax.numpy as jnp
from jax import lax
from jax.experimental import pallas as pl
from jax.experimental.pallas import tpu as pltpu
from jax.sharding import PartitionSpec as P

MESH = pl.DeviceIdType.MESH
F32 = jnp.float32
BF16 = jnp.bfloat16
LANE = 128
SEGS = 8


def grid_of(ctx):
    z = {32: 8, 4: 2, 8: 4}[ctx]
    return ctx // z, z


def cmul(ar, ai, br, bi):
    return ar * br - ai * bi, ar * bi + ai * br


def wide(row, states):
    return jnp.concatenate([row] * (states // LANE), axis=1)


def lanes_of(j):
    return slice(j * LANE, (j + 1) * LANE)


def nearest_last(n):
    return sorted(range(1, n), key=lambda k: -min(k, n - k))


def kernel(
    dims,
    starts_ref, blocks_ref, mod_ref, phase_ref, gain_ref, retain_ref, u_hbm, cot_hbm, w_hbm,
    gin_ref, gproj_ref, geig_ref, ggain_ref,
    u_raw, cot_raw, w_raw, w_wide, w_ref, mask,
    ur, ui, st_r, st_i, sg_r, sg_i, seg, bseg, carry_f, carry_b,
    cga, cslab, ps_send, ps_recv, half, sga, grads, out_p, recv_p, out_z, recv_z,
    msg_fz, msg_fx, msg_bz, msg_bx, msg_sy,
    load_s, slab_s, slab_r, ag_s, ag_r, dd_s, dd_r, ps_s, ps_r, sg_s, sg_rs,
    p_s, p_r, z_s, z_r,
    fz_s, fz_r, fx_s, fx_r, bz_s, bz_r, bx_s, bx_r, sy_s, sy_r,
):
    ny, nx, nz, nc = dims
    tokens, width = cot_raw.shape
    tiles = ur.shape[0]
    states = tiles * LANE
    steps = tokens // SEGS
    slab = width // ny
    stages = ny // nc
    y = lax.axis_index("dp")
    ctx = lax.axis_index("ctx")
    c = lax.axis_index("chan")
    x, z = ctx // nz, ctx % nz

    def at_z(other):
        return (y, x * nz + other, c)

    def at_x(other):
        return (y, other * nz + z, c)

    def at_y(other):
        return (other, ctx, c)

    def at_yx(row, col):
        return (row, col * nz + z, c)

    sibling = (y, ctx, 1 - c)
    z_peers = [(z + k) % nz for k in nearest_last(nz)]
    x_peers = [(x + k) % nx for k in nearest_last(nx)]
    y_peers = [(y + k) % ny for k in nearest_last(ny)]

    yx_peers = [(p, q) for p in y_peers for q in x_peers]

    def copy(src, dst, ssem, rsem, device):
        return pltpu.make_async_remote_copy(
            src_ref=src, dst_ref=dst, send_sem=ssem, recv_sem=rsem,
            device_id=device, device_id_type=MESH,
        )

    barrier = pltpu.get_barrier_semaphore()
    greeted = [at_z(p) for p in z_peers] + [at_x(p) for p in x_peers]
    greeted += [at_y(p) for p in y_peers] + [sibling] + [at_yx(*p) for p in yx_peers]
    for device in greeted:
        pl.semaphore_signal(barrier, inc=1, device_id=device, device_id_type=MESH)
    load_cot = pltpu.make_async_copy(cot_hbm, cot_raw, load_s.at[0])
    load_u = pltpu.make_async_copy(u_hbm, u_raw, load_s.at[1])
    load_w = pltpu.make_async_copy(w_hbm, w_raw, load_s.at[2])
    load_cot.start()
    load_u.start()
    load_w.start()

    alive = jnp.where(ctx < blocks_ref[...], 1.0, 0.0)
    alive = jnp.broadcast_to(alive, (tokens, slab)).astype(BF16)
    load_cot.wait()
    for q in range(ny):
        cga[z, q] = cot_raw[:, q * slab:(q + 1) * slab] * alive
    pl.semaphore_wait(barrier, len(greeted))

    def arrived(view, rsem):
        copy(view, view, rsem, rsem, sibling).wait_recv()

    def departed(view, ssem):
        pending.append(copy(view, view, ssem, ssem, sibling))

    def settle():
        for s in pending:
            s.wait_send()
        pending.clear()

    def spread(buf, ssem, rsem, mine, peers, where):
        for p in peers:
            copy(buf.at[mine], buf.at[mine], ssem, rsem, where(p)).start()
        if peers:
            departed(buf.at[pl.ds(0, len(peers))], ssem)

    def collect(buf, rsem, peers):
        if peers:
            arrived(buf.at[pl.ds(0, len(peers))], rsem)

    pending = []

    for p in y_peers:
        copy(cga.at[z, p], cslab.at[y], slab_s, slab_r.at[y], at_y(p)).start()
    departed(cslab.at[pl.ds(0, ny - 1)], slab_s)

    n_right = nz // 2
    n_left = nz - 1 - n_right

    def ring_step(stage, k):
        q = stage * nc + c
        for way, count in ((0, n_right), (1, n_left)):
            sign = -1 if way == 0 else 1
            slot = (z + sign * k) % nz
            view = cga.at[slot, q]
            if 1 <= k <= count:
                arrived(view, ag_r.at[stage, slot])
            if k < count:
                copy(view, view, ag_s.at[stage], ag_r.at[stage, slot], at_z((z - sign) % nz)).start()
            if 1 <= k <= count:
                copy(view, view, dd_s.at[stage], dd_r.at[stage], sibling).start()
        if k == n_right:
            departed(cga.at[pl.ds(0, nz - 1), q], ag_s.at[stage])
            departed(cga.at[pl.ds(0, nz - 1), q], dd_s.at[stage])

    def ring_end(stage):
        arrived(cga.at[pl.ds(0, nz - 1), stage * nc + 1 - c], dd_r.at[stage])

    todo = sorted(
        [(stage, k) for k in range(n_right + 1) for stage in range(stages)],
        key=lambda step: (step[0] + step[1], step[0]),
    )

    def advance(count=1):
        for _ in range(min(count, len(todo))):
            ring_step(*todo.pop(0))

    advance()

    load_w.wait()
    depth = w_wide.shape[1]

    def part_weights(n, carry):
        at = pl.ds(pl.multiple_of(n * depth, depth), depth)
        block = w_raw[at].astype(F32)
        w_wide[0] = block[:, 0, :]
        w_wide[1] = block[:, 1, :]
        w_ref[0, at, :] = w_wide[0].astype(BF16)
        w_ref[1, at, :] = w_wide[1].astype(BF16)
        return carry

    parts = slab // depth
    lax.fori_loop(0, parts, part_weights, 0)
    advance(2)

    row = lax.broadcasted_iota(jnp.int32, (1, tokens), 1) + ctx * tokens
    keep = retain_ref[...]
    for k in range(starts_ref.shape[1]):
        keep = jnp.where(row == starts_ref[0, k], 0.0, keep)
    mask[...] = jnp.broadcast_to(keep, (LANE, tokens)).T

    lr1 = mod_ref[...] * jnp.cos(phase_ref[...])
    li1 = mod_ref[...] * jnp.sin(phase_ref[...])
    shape = (SEGS, states)
    lr = jnp.broadcast_to(lr1, shape)
    li = jnp.broadcast_to(li1, shape)
    gain = jnp.broadcast_to(gain_ref[...], shape)

    def power(br, bi, n):
        while n > 1:
            br, bi = cmul(br, bi, br, bi)
            n //= 2
        return br, bi

    seg_r, seg_i = power(lr1, li1, steps)
    blk_r, blk_i = power(seg_r, seg_i, SEGS)
    row_r, row_i = power(blk_r, blk_i, nz)

    load_u.wait()
    drive = u_raw[...].astype(F32)
    for j in range(tiles):
        ur[j] = drive[:, 0, lanes_of(j)]
        ui[j] = drive[:, 1, lanes_of(j)]

    def rows(ref, i):
        at = pl.ds(i, SEGS, stride=steps)
        return jnp.concatenate([ref[j, at, :] for j in range(tiles)], axis=1)

    def put_rows(ref, i, value):
        for j in range(tiles):
            ref[j, pl.ds(i, SEGS, stride=steps), :] = value[:, lanes_of(j)]

    def keep_at(i):
        return mask[pl.ds(i, SEGS, stride=steps), :]

    def summary(i, held):
        sr, si, kp = held
        k = keep_at(i)
        kk = wide(k, states)
        tr, ti = cmul(lr, li, sr, si)
        return kk * tr + gain * rows(ur, i), kk * ti + gain * rows(ui, i), kp * k

    zero = jnp.zeros(shape, F32)
    sr, si, kp = lax.fori_loop(0, steps, summary, (zero, zero, jnp.ones((SEGS, LANE), F32)))
    seg[0] = sr
    seg[1] = si
    seg[2] = wide(kp, states)

    def chain(hr, hi, sign, hold):
        order = range(SEGS) if sign > 0 else range(SEGS - 1, -1, -1)
        for g in order:
            if hold is not None:
                hold[0, g:g + 1] = hr
                hold[1, g:g + 1] = hi
            pr, pi = cmul(seg_r, sign * seg_i, hr, hi)
            kg = seg[2, g:g + 1]
            hr = kg * pr + seg[0, g:g + 1]
            hi = kg * pi + seg[1, g:g + 1]
        return hr, hi

    one = jnp.ones((1, states), F32)
    nil = jnp.zeros((1, states), F32)

    def across(buf, mine, n, ar, ai, sign, keeps):
        order = range(n) if sign > 0 else range(n - 1, -1, -1)
        hr, hi, pr, pi, kr = nil, nil, one, nil, one[:, :LANE]
        er, ei, qr, qi = nil, nil, one, nil
        for k in order:
            here = k == mine
            er = jnp.where(here, hr, er)
            ei = jnp.where(here, hi, ei)
            qr = jnp.where(here, pr, qr)
            qi = jnp.where(here, pi, qi)
            kw = wide(keeps[k], states)
            mr, mi = cmul(ar, sign * ai, hr, hi)
            hr = kw * mr + buf[k, :, 0:states]
            hi = kw * mi + buf[k, :, states:2 * states]
            mr, mi = cmul(ar, sign * ai, pr, pi)
            pr, pi = kw * mr, kw * mi
            kr = kr * keeps[k]
        return hr, hi, er, ei, qr, qi, kr

    br, bi = chain(nil, nil, 1, None)
    kb = one[:, :LANE]
    for g in range(SEGS):
        kb = kb * seg[2, g:g + 1, 0:LANE]
    msg_fz[z, :, 0:states] = br
    msg_fz[z, :, states:2 * states] = bi
    msg_fz[z, :, 2 * states:] = kb
    spread(msg_fz, fz_s, fz_r, z, z_peers, at_z)

    for p in y_peers:
        arrived(cslab.at[p], slab_r.at[p])
        for h in range(2):
            ps_send[p, h] = jnp.dot(cslab[p], w_ref[h], preferred_element_type=F32).astype(BF16)
            copy(ps_send.at[p, h], ps_recv.at[y, h], ps_s, ps_r, at_y(p)).start()
    departed(ps_send.at[pl.ds(0, ny - 1)], ps_s)
    advance(2)

    collect(msg_fz, fz_r, z_peers)
    keeps_z = [msg_fz[k, :, 2 * states:] for k in range(nz)]
    hr, hi, er, ei, qr, qi, kx = across(msg_fz, z, nz, blk_r, blk_i, 1, keeps_z)
    msg_fx[x, :, 0:states] = hr
    msg_fx[x, :, states:2 * states] = hi
    msg_fx[x, :, 2 * states:] = kx
    spread(msg_fx, fx_s, fx_r, x, x_peers, at_x)

    advance(2)
    own = cga[z, y]
    for h, ref in ((0, sg_r), (1, sg_i)):
        share = jnp.dot(own, w_ref[h], preferred_element_type=F32)
        for j in range(tiles):
            ref[j] = share[:, lanes_of(j)]
    collect(msg_fx, fx_r, x_peers)
    keeps_x = [msg_fx[k, :, 2 * states:] for k in range(nx)]
    _, _, fr, fi, _, _, _ = across(msg_fx, x, nx, row_r, row_i, 1, keeps_x)
    mr, mi = cmul(qr, qi, fr, fi)
    chain(mr + er, mi + ei, 1, carry_f)

    def fill(i, held):
        sr, si = held
        kk = wide(keep_at(i), states)
        tr, ti = cmul(lr, li, sr, si)
        sr = kk * tr + gain * rows(ur, i)
        si = kk * ti + gain * rows(ui, i)
        put_rows(st_r, i, sr)
        put_rows(st_i, i, si)
        return sr, si

    lax.fori_loop(0, steps, fill, (carry_f[0], carry_f[1]))
    for k in range(nz):
        half[k, :, 0:LANE] = st_r[k].astype(BF16)
        half[k, :, LANE:] = st_i[k].astype(BF16)
    for p in z_peers:
        copy(half.at[p], sga.at[z], sg_s, sg_rs, at_z(p)).start()
    departed(half.at[pl.ds(0, nz - 1)], sg_s)
    sga[z] = half[z]
    advance(2)


    def project(stage):
        count = nz * tokens
        state_t = sga[...].reshape(count, 2 * LANE).T
        for q in range(stage * nc, (stage + 1) * nc):
            block = cga[:, q].reshape(count, slab)
            grad = jnp.dot(state_t, block, preferred_element_type=F32)
            for k in range(nx):
                grads[q, k] = grad[:, lanes_of(k)]
                out_p[q * nx + k] = grad[:, lanes_of(k)].astype(BF16)
                s = copy(out_p.at[q * nx + k], recv_p.at[y * nx + x], p_s, p_r, at_yx(q, k))
                pl.when((q != y) | (k != x))(s.start)

    ring_end(0)
    collect(sga, sg_rs, z_peers)
    project(0)
    advance(len(todo))

    arrived(ps_recv.at[pl.ds(0, ny - 1)], ps_r)
    for p in y_peers:
        for h, ref in ((0, sg_r), (1, sg_i)):
            for j in range(tiles):
                ref[j] += ps_recv[p, h, :, lanes_of(j)].astype(F32)

    def some(ref, i, group):
        at = pl.ds(i, SEGS, stride=steps)
        return jnp.concatenate([ref[j, at, :] for j in group], axis=1)

    def back_step(group, i, held, prior_r, prior_i):
        hr, hi, tr, ti, wr, wi, qr, qi, wg, rr, ri = held
        cols = slice(group[0] * LANE, (group[-1] + 1) * LANE)
        kk = wide(keep_at(i), len(group) * LANE)
        vr, vi = some(ur, i, group), some(ui, i, group)
        xr, xi = some(sg_r, i, group) + hr, some(sg_i, i, group) + hi
        pr, pi = kk * prior_r, kk * prior_i
        wr, wi = wr + (xr * pr + xi * pi), wi + (xi * pr - xr * pi)
        qr, qi = qr + (tr * pr + ti * pi), qi + (ti * pr - tr * pi)
        wg = wg + (xr * vr + xi * vi)
        rr, ri = rr + (tr * vr + ti * vi), ri + (ti * vr - tr * vi)
        ar, ai = kk * lr[:, cols], kk * -li[:, cols]
        hr, hi = cmul(ar, ai, xr, xi)
        tr, ti = cmul(ar, ai, tr, ti)
        return hr, hi, tr, ti, wr, wi, qr, qi, wg, rr, ri

    span = max(1, tiles // 4)
    for first in range(0, tiles, span):
        group = range(first, first + span)
        cols = slice(first * LANE, (first + span) * LANE)
        none = jnp.zeros((SEGS, span * LANE), F32)
        held = (none, none, none + 1.0) + (none,) * 8

        def back(n, held, group=group):
            i = steps - 1 - n
            return back_step(group, i, held, some(st_r, i - 1, group), some(st_i, i - 1, group))

        held = lax.fori_loop(0, steps - 1, back, held)
        held = back_step(group, 0, held, carry_f[0, :, cols], carry_f[1, :, cols])
        for k, value in enumerate(held):
            bseg[k, :, cols] = value

    def fold(held, parts, link):
        hr, hi, pr, pi, wr, wi, qr, qi, wg, rr, ri = held
        br, bi, vr, vi, sr, si, sg, ur_, ui_ = parts
        mr, mi = cmul(sr, si, hr, hi)
        wr, wi = wr + (vr + mr), wi + (vi + mi)
        mr, mi = cmul(sr, si, pr, pi)
        qr, qi = qr + mr, qi + mi
        wg = wg + (sg + (ur_ * hr - ui_ * hi))
        mr, mi = cmul(ur_, ui_, pr, pi)
        rr, ri = rr + mr, ri + mi
        mr, mi = cmul(*link, hr, hi)
        hr, hi = mr + br, mi + bi
        pr, pi = cmul(*link, pr, pi)
        return hr, hi, pr, pi, wr, wi, qr, qi, wg, rr, ri

    fresh = (nil, nil, one) + (nil,) * 8

    def row_of(k, g):
        return bseg[k, g:g + 1]

    held = fresh
    for g in range(SEGS - 1, -1, -1):
        for k in range(4):
            carry_b[k, g:g + 1] = held[k]
        parts = [row_of(k, g) for k in (0, 1, 4, 5, 6, 7, 8, 9, 10)]
        held = fold(held, parts, (row_of(2, g), row_of(3, g)))

    def put(buf, mine, values):
        for k, value in enumerate(values):
            buf[mine, :, k * states:(k + 1) * states] = value

    def join(buf, mine, n, ar, ai, keeps):
        held = fresh
        mark = fresh[:4]
        for k in range(n - 1, -1, -1):
            here = k == mine
            mark = [jnp.where(here, new, old) for new, old in zip(held[:4], mark)]
            kw = wide(keeps[k], states)
            parts = [buf[k, :, m * states:(m + 1) * states] for m in range(9)]
            held = fold(held, parts, (kw * ar, kw * -ai))
        return held, mark

    put(msg_bz, z, held[:2] + held[4:])
    spread(msg_bz, bz_s, bz_r, z, z_peers, at_z)
    for stage in range(1, stages):
        ring_end(stage)
        project(stage)
    collect(msg_bz, bz_r, z_peers)
    held, (er, ei, qr, qi) = join(msg_bz, z, nz, blk_r, blk_i, keeps_z)
    put(msg_bx, x, held[:2] + held[4:])
    spread(msg_bx, bx_s, bx_r, x, x_peers, at_x)
    settle()
    collect(msg_bx, bx_r, x_peers)
    held, (fr, fi, _, _) = join(msg_bx, x, nx, row_r, row_i, keeps_x)
    put(msg_sy, y, (held[4], held[5], held[8]))
    spread(msg_sy, sy_s, sy_r, y, y_peers, at_y)
    mr, mi = cmul(qr, qi, fr, fi)
    mr, mi = cmul(carry_b[2], carry_b[3], mr + er, mi + ei)

    def adjoint(n, held):
        i = steps - 1 - n
        hr, hi = held
        kk = wide(keep_at(i), states)
        ar = rows(sg_r, i) + hr
        ai = rows(sg_i, i) + hi
        put_rows(sg_r, i, gain * ar)
        put_rows(sg_i, i, gain * ai)
        tr, ti = cmul(lr, -li, ar, ai)
        return kk * tr, kk * ti

    lax.fori_loop(0, steps, adjoint, (carry_b[0] + mr, carry_b[1] + mi))
    for h, ref in ((0, sg_r), (1, sg_i)):
        gin_ref[:, h, :] = jnp.concatenate([ref[j].astype(BF16) for j in range(tiles)], axis=1)

    arrived(recv_p.at[pl.ds(0, ny * nx - 1)], p_r)
    departed(out_p.at[pl.ds(0, ny * nx - 1)], p_s)
    grad = grads[y, x]
    for p, q in [(y, q) for q in x_peers] + [(p, x) for p in y_peers] + yx_peers:
        grad = grad + recv_p[p * nx + q].astype(F32)
    out_z[...] = grad.T.reshape(out_z.shape)
    for p in z_peers:
        copy(out_z.at[p], recv_z.at[z], z_s, z_r, at_z(p)).start()
    departed(out_z.at[pl.ds(0, nz - 1)], z_s)
    recv_z[z] = out_z[z]

    collect(msg_sy, sy_r, y_peers)
    sums = msg_sy[0]
    for k in range(1, ny):
        sums = sums + msg_sy[k]
    geig_ref[0:1] = sums[:, 0:states]
    geig_ref[1:2] = sums[:, states:2 * states]
    ggain_ref[...] = sums[:, 2 * states:]

    collect(recv_z, z_r, z_peers)
    for k in range(nz):
        for h in range(2):
            gproj_ref[:, h, lanes_of(k)] = recv_z[k, :, lanes_of(h)]

    settle()


def hand_over(*refs):
    count = len(refs) // 2
    for k in range(count):
        refs[count + k][...] = refs[k][...]


def body(dims, inputs, cotangent, out_proj, modulus, phase, gain, retain, doc_starts, row_blocks):
    ny, nx, nz, nc = dims
    _, tokens, _, states = inputs.shape
    width = cotangent.shape[2]
    slab = width // ny
    stages = ny // nc
    rows_z = LANE // nz
    dma = pltpu.SemaphoreType.DMA

    line = 2 * states + LANE
    scratch = [
        pltpu.VMEM((tokens, 2, states), BF16),
        pltpu.VMEM((tokens, width), BF16),
        pltpu.VMEM((slab, 2, states), BF16),
        pltpu.VMEM((2, LANE, states), F32),
        pltpu.VMEM((2, slab, states), BF16),
        pltpu.VMEM((tokens, LANE), F32),
        *[pltpu.VMEM((states // LANE, tokens, LANE), F32) for _ in range(6)],
        pltpu.VMEM((3, SEGS, states), F32),
        pltpu.VMEM((11, SEGS, states), F32),
        pltpu.VMEM((2, SEGS, states), F32), pltpu.VMEM((4, SEGS, states), F32),
        pltpu.VMEM((nz, ny, tokens, slab), BF16),
        pltpu.VMEM((ny, tokens, slab), BF16),
        pltpu.VMEM((ny, 2, tokens, states), BF16), pltpu.VMEM((ny, 2, tokens, states), BF16),
        pltpu.VMEM((nz, tokens, 2 * LANE), BF16), pltpu.VMEM((nz, tokens, 2 * LANE), BF16),
        pltpu.VMEM((ny, nx, 2 * LANE, LANE), F32),
        pltpu.VMEM((ny * nx, 2 * LANE, LANE), BF16), pltpu.VMEM((ny * nx, 2 * LANE, LANE), BF16),
        pltpu.VMEM((nz, rows_z, 2 * LANE), F32), pltpu.VMEM((nz, rows_z, 2 * LANE), F32),
        pltpu.VMEM((nz, 1, line), F32), pltpu.VMEM((nx, 1, line), F32),
        pltpu.VMEM((nz, 1, 9 * states), F32), pltpu.VMEM((nx, 1, 9 * states), F32),
        pltpu.VMEM((ny, 1, 3 * states), F32),
        dma((3,)), dma, dma((ny,)), dma((stages,)), dma((stages, nz)), dma((stages,)), dma((stages,)),
        *[dma for _ in range(8)],
        *[dma for _ in range(10)],
    ]
    vmem = pl.BlockSpec(memory_space=pltpu.VMEM)
    smem = pl.BlockSpec(memory_space=pltpu.SMEM)
    hbm = pl.BlockSpec(memory_space=pl.ANY)
    results = pl.pallas_call(
        functools.partial(kernel, dims),
        out_shape=(
            jax.ShapeDtypeStruct((tokens, 2, states), BF16),
            jax.ShapeDtypeStruct((rows_z, 2, states), F32),
            jax.ShapeDtypeStruct((2, states), F32),
            jax.ShapeDtypeStruct((1, states), F32),
        ),
        in_specs=[smem, vmem, vmem, vmem, vmem, vmem, hbm, hbm, hbm],
        out_specs=(vmem,) * 4,
        scratch_shapes=scratch,
        compiler_params=pltpu.CompilerParams(
            collective_id=0, has_side_effects=True, vmem_limit_bytes=56 * 1024 * 1024
        ),
    )(
        doc_starts, row_blocks[None], modulus[None], phase[None], gain[None], retain,
        inputs[0], cotangent[0], out_proj,
    )
    grad_inputs, grad_proj, grad_eigen, grad_gain = pl.pallas_call(
        hand_over,
        out_shape=tuple(jax.ShapeDtypeStruct(r.shape, r.dtype) for r in results),
        in_specs=[vmem] * 4,
        out_specs=(vmem,) * 4,
    )(*results)
    return grad_inputs[None], grad_proj, grad_eigen, grad_gain[0]


def solution(mesh):
    sizes = mesh.shape
    nx, nz = grid_of(sizes["ctx"])
    dims = (sizes["dp"], nx, nz, sizes["chan"])
    return jax.shard_map(
        functools.partial(body, dims),
        mesh=mesh,
        in_specs=(
            P("dp", "ctx", None, "chan"),
            P("dp", "ctx", None),
            P("dp", None, "chan"),
            P("chan"),
            P("chan"),
            P("chan"),
            P("dp", "ctx"),
            P("dp", None),
            P("dp"),
        ),
        out_specs=(
            P("dp", "ctx", None, "chan"),
            P(("dp", "ctx"), None, "chan"),
            P(None, "chan"),
            P("chan"),
        ),
        check_vma=False,
    )
```

time: 91 us -> 73.2 us (0.80)
  Pallas kernels: 81.9 us -> 71.2 us
  local copies, waits for them, and re-layouts: 6.32 us -> 0 us
    pallas_call x1, Pallas kernels: 81.9 us -> 69.2 us  [body(): pl.pallas_call(functools.partial(kernel, dims), out_shape=(jax.ShapeDtype...]
    unnamed x4 -> x0, local copies, waits for them, and re-layouts: 6.32 us -> none
    pallas_call x0 -> x1, Pallas kernels: none -> 1.97 us  [body(): pl.pallas_call(hand_over, out_shape=tuple((jax.ShapeDtypeStruct(r.shape,...]
where the time goes in v3:
time: 73.2 us; the launch traced here: 72.5 us
  Pallas kernels  71.2 us (97%)
  between operations  1.29 us (2%)
    pallas_call x1, Pallas kernels, body(): pl.pallas_call(functools.partial(kernel, dims), out_shape=(jax.ShapeDtype...  69.2 us
    pallas_call x1, Pallas kernels, body(): pl.pallas_call(hand_over, out_shape=tuple((jax.ShapeDtypeStruct(r.shape,...  1.97 us

profile of v3, /device:TPU:32, one launch (start us, length us, event | category | flops | bytes accessed | tf_op | source)
XLA Modules:
  0.0 72.5 jit_solution(17604621977423726843)
XLA Ops:
  1.3 69.2 %shard_map.120 = (bf16[128,2,1024]{2,1,0:T(2,128)(2,1)}, f32[16,2,1024]{2,1,0:T(2,128)}, f32[2,1024]{1,0:T(2,128)}, f32[1,1024]{1,0:T(1,128)}) custom-call(s32[1,8]{1,0:T(1,128)} %starts_ref.1, s32[1,1]{1,0:T(1,128)} %bitcast.8.blocks_ref, f32[1,1024]{1,0:T(1,128)} %bitcast.11, f32[1,1024]{1,0:T(1,128)} %bitcast.12, f32[1,1024]{1,0:T(1,128)} %bitcast.13, ...), custom_call_target="tpu_custom_call" | custom-call | tf_op jit(solution)/shard_map/pallas_call | solution.py:531
  70.5 2.0 %shard_map.121 = (bf16[128,2,1024]{2,1,0:T(2,128)(2,1)}, f32[16,2,1024]{2,1,0:T(2,128)}, f32[2,1024]{1,0:T(2,128)}, f32[1,1024]{1,0:T(1,128)}) custom-call(bf16[128,2,1024]{2,1,0:T(2,128)(2,1)} %get-tuple-element.12.refs_0_, f32[16,2,1024]{2,1,0:T(2,128)} %get-tuple-element.13.refs_1_, f32[2,1024]{1,0:T(2,128)} %get-tuple-element.14.refs_2_, ...), custom_call_target="tpu_custom_call" | custom-call | tf_op jit(solution)/shard_map/pallas_call | solution.py:549

commit v4 on v3

--- a/solution.py
+++ b/solution.py
@@ -41,10 +41,10 @@
     gin_ref, gproj_ref, geig_ref, ggain_ref,
     u_raw, cot_raw, w_raw, w_wide, w_ref, mask,
     ur, ui, st_r, st_i, sg_r, sg_i, seg, bseg, carry_f, carry_b,
-    cga, cslab, ps_send, ps_recv, half, sga, grads, out_p, recv_p, out_z, recv_z,
+    cga, cslab, ps_send, ps_recv, half, sga, state_t, grads, out_x, recv_x, out_y, recv_y, out_z, recv_z,
     msg_fz, msg_fx, msg_bz, msg_bx, msg_sy,
     load_s, slab_s, slab_r, ag_s, ag_r, dd_s, dd_r, ps_s, ps_r, sg_s, sg_rs,
-    p_s, p_r, z_s, z_r,
+    x_s, x_r, y_s, y_r, z_s, z_r,
     fz_s, fz_r, fx_s, fx_r, bz_s, bz_r, bx_s, bx_r, sy_s, sy_r,
 ):
     ny, nx, nz, nc = dims
@@ -68,15 +68,10 @@
     def at_y(other):
         return (other, ctx, c)
 
-    def at_yx(row, col):
-        return (row, col * nz + z, c)
-
     sibling = (y, ctx, 1 - c)
     z_peers = [(z + k) % nz for k in nearest_last(nz)]
     x_peers = [(x + k) % nx for k in nearest_last(nx)]
     y_peers = [(y + k) % ny for k in nearest_last(ny)]
-
-    yx_peers = [(p, q) for p in y_peers for q in x_peers]
 
     def copy(src, dst, ssem, rsem, device):
         return pltpu.make_async_remote_copy(
@@ -86,7 +81,7 @@
 
     barrier = pltpu.get_barrier_semaphore()
     greeted = [at_z(p) for p in z_peers] + [at_x(p) for p in x_peers]
-    greeted += [at_y(p) for p in y_peers] + [sibling] + [at_yx(*p) for p in yx_peers]
+    greeted += [at_y(p) for p in y_peers] + [sibling]
     for device in greeted:
         pl.semaphore_signal(barrier, inc=1, device_id=device, device_id_type=MESH)
     load_cot = pltpu.make_async_copy(cot_hbm, cot_raw, load_s.at[0])
@@ -130,22 +125,29 @@
         copy(cga.at[z, p], cslab.at[y], slab_s, slab_r.at[y], at_y(p)).start()
     departed(cslab.at[pl.ds(0, ny - 1)], slab_s)
 
-    n_right = nz // 2
-    n_left = nz - 1 - n_right
+    hops = nz // 2
+    split = tokens // 2
+
+    def ring_part(slot, q, k, way):
+        if k < hops or nz % 2:
+            return cga.at[slot, q]
+        return cga.at[slot, q, pl.ds(way * split, split)]
 
     def ring_step(stage, k):
         q = stage * nc + c
-        for way, count in ((0, n_right), (1, n_left)):
+        for way in range(2):
             sign = -1 if way == 0 else 1
             slot = (z + sign * k) % nz
-            view = cga.at[slot, q]
-            if 1 <= k <= count:
-                arrived(view, ag_r.at[stage, slot])
-            if k < count:
-                copy(view, view, ag_s.at[stage], ag_r.at[stage, slot], at_z((z - sign) % nz)).start()
-            if 1 <= k <= count:
-                copy(view, view, dd_s.at[stage], dd_r.at[stage], sibling).start()
-        if k == n_right:
+            if k >= 1:
+                arrived(ring_part(slot, q, k, way), ag_r.at[stage, way, k])
+            if k < hops:
+                part = ring_part(slot, q, k + 1, way)
+                to = at_z((z - sign) % nz)
+                copy(part, part, ag_s.at[stage], ag_r.at[stage, way, k + 1], to).start()
+            if k >= 1:
+                part = ring_part(slot, q, k, way)
+                copy(part, part, dd_s.at[stage], dd_r.at[stage], sibling).start()
+        if k == hops:
             departed(cga.at[pl.ds(0, nz - 1), q], ag_s.at[stage])
             departed(cga.at[pl.ds(0, nz - 1), q], dd_s.at[stage])
 
@@ -153,7 +155,7 @@
         arrived(cga.at[pl.ds(0, nz - 1), stage * nc + 1 - c], dd_r.at[stage])
 
     todo = sorted(
-        [(stage, k) for k in range(n_right + 1) for stage in range(stages)],
+        [(stage, k) for k in range(hops + 1) for stage in range(stages)],
         key=lambda step: (step[0] + step[1], step[0]),
     )
 
@@ -162,22 +164,6 @@
             ring_step(*todo.pop(0))
 
     advance()
-
-    load_w.wait()
-    depth = w_wide.shape[1]
-
-    def part_weights(n, carry):
-        at = pl.ds(pl.multiple_of(n * depth, depth), depth)
-        block = w_raw[at].astype(F32)
-        w_wide[0] = block[:, 0, :]
-        w_wide[1] = block[:, 1, :]
-        w_ref[0, at, :] = w_wide[0].astype(BF16)
-        w_ref[1, at, :] = w_wide[1].astype(BF16)
-        return carry
-
-    parts = slab // depth
-    lax.fori_loop(0, parts, part_weights, 0)
-    advance(2)
 
     row = lax.broadcasted_iota(jnp.int32, (1, tokens), 1) + ctx * tokens
     keep = retain_ref[...]
@@ -275,6 +261,22 @@
     msg_fz[z, :, 2 * states:] = kb
     spread(msg_fz, fz_s, fz_r, z, z_peers, at_z)
 
+    advance(2)
+    load_w.wait()
+    depth = w_wide.shape[1]
+
+    def part_weights(n, carry):
+        at = pl.ds(pl.multiple_of(n * depth, depth), depth)
+        block = w_raw[at].astype(F32)
+        w_wide[0] = block[:, 0, :]
+        w_wide[1] = block[:, 1, :]
+        w_ref[0, at, :] = w_wide[0].astype(BF16)
+        w_ref[1, at, :] = w_wide[1].astype(BF16)
+        return carry
+
+    parts = slab // depth
+    lax.fori_loop(0, parts, part_weights, 0)
+
     for p in y_peers:
         arrived(cslab.at[p], slab_r.at[p])
         for h in range(2):
@@ -326,15 +328,16 @@
 
     def project(stage):
         count = nz * tokens
-        state_t = sga[...].reshape(count, 2 * LANE).T
+        if stage == 0:
+            state_t[...] = sga[...].reshape(count, 2 * LANE).T
         for q in range(stage * nc, (stage + 1) * nc):
             block = cga[:, q].reshape(count, slab)
-            grad = jnp.dot(state_t, block, preferred_element_type=F32)
+            grad = jnp.dot(state_t[...], block, preferred_element_type=F32)
             for k in range(nx):
                 grads[q, k] = grad[:, lanes_of(k)]
-                out_p[q * nx + k] = grad[:, lanes_of(k)].astype(BF16)
-                s = copy(out_p.at[q * nx + k], recv_p.at[y * nx + x], p_s, p_r, at_yx(q, k))
-                pl.when((q != y) | (k != x))(s.start)
+                out_x[k, q] = grad[:, lanes_of(k)].astype(BF16)
+            for p in x_peers:
+                copy(out_x.at[p, q], recv_x.at[x, q], x_s, x_r, at_x(p)).start()
 
     ring_end(0)
     collect(sga, sg_rs, z_peers)
@@ -434,6 +437,17 @@
     held, (er, ei, qr, qi) = join(msg_bz, z, nz, blk_r, blk_i, keeps_z)
     put(msg_bx, x, held[:2] + held[4:])
     spread(msg_bx, bx_s, bx_r, x, x_peers, at_x)
+    if nx > 1:
+        arrived(recv_x.at[pl.ds(0, nx - 1)], x_r)
+        departed(out_x.at[pl.ds(0, nx - 1)], x_s)
+    for q in range(ny):
+        grad = grads[q, x]
+        for p in x_peers:
+            grad = grad + recv_x[p, q].astype(F32)
+        grads[q, 0] = grad
+        out_y[q] = grad.astype(BF16)
+    for p in y_peers:
+        copy(out_y.at[p], recv_y.at[y], y_s, y_r, at_y(p)).start()
     settle()
     collect(msg_bx, bx_r, x_peers)
     held, (fr, fi, _, _) = join(msg_bx, x, nx, row_r, row_i, keeps_x)
@@ -457,11 +471,12 @@
     for h, ref in ((0, sg_r), (1, sg_i)):
         gin_ref[:, h, :] = jnp.concatenate([ref[j].astype(BF16) for j in range(tiles)], axis=1)
 
-    arrived(recv_p.at[pl.ds(0, ny * nx - 1)], p_r)
-    departed(out_p.at[pl.ds(0, ny * nx - 1)], p_s)
-    grad = grads[y, x]
-    for p, q in [(y, q) for q in x_peers] + [(p, x) for p in y_peers] + yx_peers:
-        grad = grad + recv_p[p * nx + q].astype(F32)
+    if ny > 1:
+        arrived(recv_y.at[pl.ds(0, ny - 1)], y_r)
+        departed(out_y.at[pl.ds(0, ny - 1)], y_s)
+    grad = grads[y, 0]
+    for p in y_peers:
+        grad = grad + recv_y[p].astype(F32)
     out_z[...] = grad.T.reshape(out_z.shape)
     for p in z_peers:
         copy(out_z.at[p], recv_z.at[z], z_s, z_r, at_z(p)).start()
@@ -515,14 +530,16 @@
         pltpu.VMEM((ny, tokens, slab), BF16),
         pltpu.VMEM((ny, 2, tokens, states), BF16), pltpu.VMEM((ny, 2, tokens, states), BF16),
         pltpu.VMEM((nz, tokens, 2 * LANE), BF16), pltpu.VMEM((nz, tokens, 2 * LANE), BF16),
+        pltpu.VMEM((2 * LANE, nz * tokens), BF16),
         pltpu.VMEM((ny, nx, 2 * LANE, LANE), F32),
-        pltpu.VMEM((ny * nx, 2 * LANE, LANE), BF16), pltpu.VMEM((ny * nx, 2 * LANE, LANE), BF16),
+        pltpu.VMEM((nx, ny, 2 * LANE, LANE), BF16), pltpu.VMEM((nx, ny, 2 * LANE, LANE), BF16),
+        pltpu.VMEM((ny, 2 * LANE, LANE), BF16), pltpu.VMEM((ny, 2 * LANE, LANE), BF16),
         pltpu.VMEM((nz, rows_z, 2 * LANE), F32), pltpu.VMEM((nz, rows_z, 2 * LANE), F32),
         pltpu.VMEM((nz, 1, line), F32), pltpu.VMEM((nx, 1, line), F32),
         pltpu.VMEM((nz, 1, 9 * states), F32), pltpu.VMEM((nx, 1, 9 * states), F32),
         pltpu.VMEM((ny, 1, 3 * states), F32),
-        dma((3,)), dma, dma((ny,)), dma((stages,)), dma((stages, nz)), dma((stages,)), dma((stages,)),
-        *[dma for _ in range(8)],
+        dma((3,)), dma, dma((ny,)), dma((stages,)), dma((stages, 2, nz)), dma((stages,)), dma((stages,)),
+        *[dma for _ in range(10)],
         *[dma for _ in range(10)],
     ]
     vmem = pl.BlockSpec(memory_space=pltpu.VMEM)

time: 73.2 us -> 70.7 us (0.966)
  Pallas kernels: 71.2 us -> 69.3 us
    pallas_call x1, Pallas kernels: 69.2 us -> 67.3 us  [body(): pl.pallas_call(functools.partial(kernel, dims), out_shape=(jax.ShapeDtype...]
where the time goes in v4:
time: 70.7 us; the launch traced here: 70.6 us
  Pallas kernels  69.3 us (98%)
  between operations  1.29 us (2%)
    pallas_call x1, Pallas kernels, body(): pl.pallas_call(functools.partial(kernel, dims), out_shape=(jax.ShapeDtype...  67.3 us
    pallas_call x1, Pallas kernels, body(): pl.pallas_call(hand_over, out_shape=tuple((jax.ShapeDtypeStruct(r.shape,...  1.97 us

profile of v4, /device:TPU:32, one launch (start us, length us, event | category | flops | bytes accessed | tf_op | source)
XLA Modules:
  0.0 70.6 jit_solution(10463236702963052497)
XLA Ops:
  1.3 67.3 %shard_map.120 = (bf16[128,2,1024]{2,1,0:T(2,128)(2,1)}, f32[16,2,1024]{2,1,0:T(2,128)}, f32[2,1024]{1,0:T(2,128)}, f32[1,1024]{1,0:T(1,128)}) custom-call(s32[1,8]{1,0:T(1,128)} %starts_ref.1, s32[1,1]{1,0:T(1,128)} %bitcast.8.blocks_ref, f32[1,1024]{1,0:T(1,128)} %bitcast.11, f32[1,1024]{1,0:T(1,128)} %bitcast.12, f32[1,1024]{1,0:T(1,128)} %bitcast.13, ...), custom_call_target="tpu_custom_call" | custom-call | tf_op jit(solution)/shard_map/pallas_call | solution.py:548
  68.6 2.0 %shard_map.121 = (bf16[128,2,1024]{2,1,0:T(2,128)(2,1)}, f32[16,2,1024]{2,1,0:T(2,128)}, f32[2,1024]{1,0:T(2,128)}, f32[1,1024]{1,0:T(1,128)}) custom-call(bf16[128,2,1024]{2,1,0:T(2,128)(2,1)} %get-tuple-element.12.refs_0_, f32[16,2,1024]{2,1,0:T(2,128)} %get-tuple-element.13.refs_1_, f32[2,1024]{1,0:T(2,128)} %get-tuple-element.14.refs_2_, ...), custom_call_target="tpu_custom_call" | custom-call | tf_op jit(solution)/shard_map/pallas_call | solution.py:566

commit v5 on v4

--- a/solution.py
+++ b/solution.py
@@ -39,7 +39,7 @@
     dims,
     starts_ref, blocks_ref, mod_ref, phase_ref, gain_ref, retain_ref, u_hbm, cot_hbm, w_hbm,
     gin_ref, gproj_ref, geig_ref, ggain_ref,
-    u_raw, cot_raw, w_raw, w_wide, w_ref, mask,
+    gin_raw, u_raw, cot_raw, w_raw, w_wide, w_ref, mask,
     ur, ui, st_r, st_i, sg_r, sg_i, seg, bseg, carry_f, carry_b,
     cga, cslab, ps_send, ps_recv, half, sga, state_t, grads, out_x, recv_x, out_y, recv_y, out_z, recv_z,
     msg_fz, msg_fx, msg_bz, msg_bx, msg_sy,
@@ -453,24 +453,6 @@
     held, (fr, fi, _, _) = join(msg_bx, x, nx, row_r, row_i, keeps_x)
     put(msg_sy, y, (held[4], held[5], held[8]))
     spread(msg_sy, sy_s, sy_r, y, y_peers, at_y)
-    mr, mi = cmul(qr, qi, fr, fi)
-    mr, mi = cmul(carry_b[2], carry_b[3], mr + er, mi + ei)
-
-    def adjoint(n, held):
-        i = steps - 1 - n
-        hr, hi = held
-        kk = wide(keep_at(i), states)
-        ar = rows(sg_r, i) + hr
-        ai = rows(sg_i, i) + hi
-        put_rows(sg_r, i, gain * ar)
-        put_rows(sg_i, i, gain * ai)
-        tr, ti = cmul(lr, -li, ar, ai)
-        return kk * tr, kk * ti
-
-    lax.fori_loop(0, steps, adjoint, (carry_b[0] + mr, carry_b[1] + mi))
-    for h, ref in ((0, sg_r), (1, sg_i)):
-        gin_ref[:, h, :] = jnp.concatenate([ref[j].astype(BF16) for j in range(tiles)], axis=1)
-
     if ny > 1:
         arrived(recv_y.at[pl.ds(0, ny - 1)], y_r)
         departed(out_y.at[pl.ds(0, ny - 1)], y_s)
@@ -483,6 +465,27 @@
     departed(out_z.at[pl.ds(0, nz - 1)], z_s)
     recv_z[z] = out_z[z]
 
+    mr, mi = cmul(qr, qi, fr, fi)
+    mr, mi = cmul(carry_b[2], carry_b[3], mr + er, mi + ei)
+
+    def adjoint(n, held):
+        i = steps - 1 - n
+        hr, hi = held
+        kk = wide(keep_at(i), states)
+        ar = rows(sg_r, i) + hr
+        ai = rows(sg_i, i) + hi
+        put_rows(sg_r, i, gain * ar)
+        put_rows(sg_i, i, gain * ai)
+        tr, ti = cmul(lr, -li, ar, ai)
+        return kk * tr, kk * ti
+
+    lax.fori_loop(0, steps, adjoint, (carry_b[0] + mr, carry_b[1] + mi))
+    for h, ref in ((0, sg_r), (1, sg_i)):
+        gin_raw[:, h, :] = jnp.concatenate([ref[j].astype(BF16) for j in range(tiles)], axis=1)
+    store_gin = pltpu.make_async_copy(gin_raw, gin_ref, load_s.at[0])
+    store_gin.start()
+
+
     collect(msg_sy, sy_r, y_peers)
     sums = msg_sy[0]
     for k in range(1, ny):
@@ -497,6 +500,7 @@
             gproj_ref[:, h, lanes_of(k)] = recv_z[k, :, lanes_of(h)]
 
     settle()
+    store_gin.wait()
 
 
 def hand_over(*refs):
@@ -516,6 +520,7 @@
 
     line = 2 * states + LANE
     scratch = [
+        pltpu.VMEM((tokens, 2, states), BF16),
         pltpu.VMEM((tokens, 2, states), BF16),
         pltpu.VMEM((tokens, width), BF16),
         pltpu.VMEM((slab, 2, states), BF16),
@@ -554,7 +559,7 @@
             jax.ShapeDtypeStruct((1, states), F32),
         ),
         in_specs=[smem, vmem, vmem, vmem, vmem, vmem, hbm, hbm, hbm],
-        out_specs=(vmem,) * 4,
+        out_specs=(hbm, vmem, vmem, vmem),
         scratch_shapes=scratch,
         compiler_params=pltpu.CompilerParams(
             collective_id=0, has_side_effects=True, vmem_limit_bytes=56 * 1024 * 1024

time: 70.7 us -> 70.6 us (level)
  no operation moved by 1% of the time
where the time goes in v5:
time: 70.6 us; the launch traced here: 70.4 us
  Pallas kernels  69.1 us (98%)
  between operations  1.29 us (2%)
    pallas_call x1, Pallas kernels, body(): pl.pallas_call(functools.partial(kernel, dims), out_shape=(jax.ShapeDtype...  67.2 us
    pallas_call x1, Pallas kernels, body(): pl.pallas_call(hand_over, out_shape=tuple((jax.ShapeDtypeStruct(r.shape,...  1.97 us

profile of v5, /device:TPU:32, one launch (start us, length us, event | category | flops | bytes accessed | tf_op | source)
XLA Modules:
  0.0 70.4 jit_solution(17986073247247197536)
XLA Ops:
  1.3 67.2 %shard_map.120 = (bf16[128,2,1024]{2,1,0:T(2,128)(2,1)}, f32[16,2,1024]{2,1,0:T(2,128)}, f32[2,1024]{1,0:T(2,128)}, f32[1,1024]{1,0:T(1,128)}) custom-call(s32[1,8]{1,0:T(1,128)} %starts_ref.1, s32[1,1]{1,0:T(1,128)} %bitcast.8.blocks_ref, f32[1,1024]{1,0:T(1,128)} %bitcast.11, f32[1,1024]{1,0:T(1,128)} %bitcast.12, f32[1,1024]{1,0:T(1,128)} %bitcast.13, ...), custom_call_target="tpu_custom_call" | custom-call | tf_op jit(solution)/shard_map/pallas_call | solution.py:553
  68.5 2.0 %shard_map.121 = (bf16[128,2,1024]{2,1,0:T(2,128)(2,1)}, f32[16,2,1024]{2,1,0:T(2,128)}, f32[2,1024]{1,0:T(2,128)}, f32[1,1024]{1,0:T(1,128)}) custom-call(bf16[128,2,1024]{2,1,0:T(2,128)(2,1)} %get-tuple-element.12.refs_0_, f32[16,2,1024]{2,1,0:T(2,128)} %get-tuple-element.13.refs_1_, f32[2,1024]{1,0:T(2,128)} %get-tuple-element.14.refs_2_, ...), custom_call_target="tpu_custom_call" | custom-call | tf_op jit(solution)/shard_map/pallas_call | solution.py:571

commit v6 on v5

--- a/solution.py
+++ b/solution.py
@@ -326,6 +326,41 @@
     advance(2)
 
 
+    def some(ref, i, group):
+        at = pl.ds(i, SEGS, stride=steps)
+        return jnp.concatenate([ref[j, at, :] for j in group], axis=1)
+
+    span = max(1, tiles // 4)
+
+    def sweep(step, count, ones, places):
+        for first in range(0, tiles, span):
+            group = range(first, first + span)
+            cols = slice(first * LANE, (first + span) * LANE)
+            none = jnp.zeros((SEGS, span * LANE), F32)
+            held = (none + 1.0,) * ones + (none,) * (count - ones)
+
+            def back(n, held, group=group):
+                i = steps - 1 - n
+                return step(group, i, held, some(st_r, i - 1, group), some(st_i, i - 1, group))
+
+            held = lax.fori_loop(0, steps - 1, back, held)
+            held = step(group, 0, held, carry_f[0, :, cols], carry_f[1, :, cols])
+            for k, value in zip(places, held):
+                bseg[k, :, cols] = value
+
+    def reach_step(group, i, held, prior_r, prior_i):
+        tr, ti, qr, qi, rr, ri = held
+        cols = slice(group[0] * LANE, (group[-1] + 1) * LANE)
+        kk = wide(keep_at(i), len(group) * LANE)
+        vr, vi = some(ur, i, group), some(ui, i, group)
+        pr, pi = kk * prior_r, kk * prior_i
+        qr, qi = qr + (tr * pr + ti * pi), qi + (ti * pr - tr * pi)
+        rr, ri = rr + (tr * vr + ti * vi), ri + (ti * vr - tr * vi)
+        tr, ti = cmul(kk * lr[:, cols], kk * -li[:, cols], tr, ti)
+        return tr, ti, qr, qi, rr, ri
+
+    sweep(reach_step, 6, 1, (2, 3, 6, 7, 9, 10))
+
     def project(stage):
         count = nz * tokens
         if stage == 0:
@@ -345,46 +380,25 @@
     advance(len(todo))
 
     arrived(ps_recv.at[pl.ds(0, ny - 1)], ps_r)
-    for p in y_peers:
-        for h, ref in ((0, sg_r), (1, sg_i)):
-            for j in range(tiles):
-                ref[j] += ps_recv[p, h, :, lanes_of(j)].astype(F32)
-
-    def some(ref, i, group):
-        at = pl.ds(i, SEGS, stride=steps)
-        return jnp.concatenate([ref[j, at, :] for j in group], axis=1)
+    for h, ref in ((0, sg_r), (1, sg_i)):
+        for j in range(tiles):
+            share = ref[j]
+            for p in y_peers:
+                share = share + ps_recv[p, h, :, lanes_of(j)].astype(F32)
+            ref[j] = share
 
     def back_step(group, i, held, prior_r, prior_i):
-        hr, hi, tr, ti, wr, wi, qr, qi, wg, rr, ri = held
+        hr, hi, wr, wi, wg = held
         cols = slice(group[0] * LANE, (group[-1] + 1) * LANE)
         kk = wide(keep_at(i), len(group) * LANE)
-        vr, vi = some(ur, i, group), some(ui, i, group)
         xr, xi = some(sg_r, i, group) + hr, some(sg_i, i, group) + hi
         pr, pi = kk * prior_r, kk * prior_i
         wr, wi = wr + (xr * pr + xi * pi), wi + (xi * pr - xr * pi)
-        qr, qi = qr + (tr * pr + ti * pi), qi + (ti * pr - tr * pi)
-        wg = wg + (xr * vr + xi * vi)
-        rr, ri = rr + (tr * vr + ti * vi), ri + (ti * vr - tr * vi)
-        ar, ai = kk * lr[:, cols], kk * -li[:, cols]
-        hr, hi = cmul(ar, ai, xr, xi)
-        tr, ti = cmul(ar, ai, tr, ti)
-        return hr, hi, tr, ti, wr, wi, qr, qi, wg, rr, ri
-
-    span = max(1, tiles // 4)
-    for first in range(0, tiles, span):
-        group = range(first, first + span)
-        cols = slice(first * LANE, (first + span) * LANE)
-        none = jnp.zeros((SEGS, span * LANE), F32)
-        held = (none, none, none + 1.0) + (none,) * 8
-
-        def back(n, held, group=group):
-            i = steps - 1 - n
-            return back_step(group, i, held, some(st_r, i - 1, group), some(st_i, i - 1, group))
-
-        held = lax.fori_loop(0, steps - 1, back, held)
-        held = back_step(group, 0, held, carry_f[0, :, cols], carry_f[1, :, cols])
-        for k, value in enumerate(held):
-            bseg[k, :, cols] = value
+        wg = wg + (xr * some(ur, i, group) + xi * some(ui, i, group))
+        hr, hi = cmul(kk * lr[:, cols], kk * -li[:, cols], xr, xi)
+        return hr, hi, wr, wi, wg
+
+    sweep(back_step, 5, 0, (0, 1, 4, 5, 8))
 
     def fold(held, parts, link):
         hr, hi, pr, pi, wr, wi, qr, qi, wg, rr, ri = held

time: 70.6 us -> 70.6 us (level)
  no operation moved by 1% of the time
where the time goes in v6:
time: 70.6 us; the launch traced here: 70.4 us
  Pallas kernels  69.1 us (98%)
  between operations  1.29 us (2%)
    pallas_call x1, Pallas kernels, body(): pl.pallas_call(functools.partial(kernel, dims), out_shape=(jax.ShapeDtype...  67.2 us
    pallas_call x1, Pallas kernels, body(): pl.pallas_call(hand_over, out_shape=tuple((jax.ShapeDtypeStruct(r.shape,...  1.97 us

profile of v6, /device:TPU:32, one launch (start us, length us, event | category | flops | bytes accessed | tf_op | source)
XLA Modules:
  0.0 70.4 jit_solution(369670228936313726)
XLA Ops:
  1.3 67.2 %shard_map.120 = (bf16[128,2,1024]{2,1,0:T(2,128)(2,1)}, f32[16,2,1024]{2,1,0:T(2,128)}, f32[2,1024]{1,0:T(2,128)}, f32[1,1024]{1,0:T(1,128)}) custom-call(s32[1,8]{1,0:T(1,128)} %starts_ref.1, s32[1,1]{1,0:T(1,128)} %bitcast.8.blocks_ref, f32[1,1024]{1,0:T(1,128)} %bitcast.11, f32[1,1024]{1,0:T(1,128)} %bitcast.12, f32[1,1024]{1,0:T(1,128)} %bitcast.13, ...), custom_call_target="tpu_custom_call" | custom-call | tf_op jit(solution)/shard_map/pallas_call | solution.py:567
  68.5 2.0 %shard_map.121 = (bf16[128,2,1024]{2,1,0:T(2,128)(2,1)}, f32[16,2,1024]{2,1,0:T(2,128)}, f32[2,1024]{1,0:T(2,128)}, f32[1,1024]{1,0:T(1,128)}) custom-call(bf16[128,2,1024]{2,1,0:T(2,128)(2,1)} %get-tuple-element.12.refs_0_, f32[16,2,1024]{2,1,0:T(2,128)} %get-tuple-element.13.refs_1_, f32[2,1024]{1,0:T(2,128)} %get-tuple-element.14.refs_2_, ...), custom_call_target="tpu_custom_call" | custom-call | tf_op jit(solution)/shard_map/pallas_call | solution.py:585
